TPU v7x, 512 devices: a whole 4x8x8 slice. The times are simulated.
512 devices in a mesh: group: 4 (over z_hi), seq: 8 (over x, z_lo), tp: 16 (over y, core).
Axes of the slice: x: 4, y: 8, z: 8 (z_hi: 4, z_lo: 2; z = z_hi * 2 + z_lo), core: 2. Of those that a mesh axis runs over, the one named last changes fastest.
Arguments:
- hidden: bfloat16 [4, 3072, 8192], P('group', 'seq', 'tp')
- passage_queries: bfloat16 [4, 3072, 8192], P('group', 'seq', 'tp')
- key_weight: bfloat16 [8192, 1024], P('tp'), may hold values from -0.0625 to 0.0625
- value_weight: bfloat16 [8192, 1024], P('tp'), may hold values from -0.0625 to 0.0625
- decode_queries: bfloat16 [4, 64, 8192], P(None, ('group', 'seq'))
- new_keys: bfloat16 [4, 64, 1024], P(None, ('group', 'seq')), may hold values from -9 to 9
- new_values: bfloat16 [4, 64, 1024], P(None, ('group', 'seq')), may hold values from -6 to 6
- cache_keys: bfloat16 [64, 2048, 1024], P(('group', 'seq'), 'tp'), may hold values from -6 to 6
- cache_values: bfloat16 [64, 2048, 1024], P(('group', 'seq'), 'tp'), may hold values from -6 to 6
- cache_lengths: int32 [64], P(('group', 'seq')), may hold values from 1 to 2048
- passage_of_row: int32 [64], P(('group', 'seq')), may hold values from 0 to 3
Outputs:
- passage_context: bfloat16 [4, 3072, 8192], P('group', 'seq', 'tp')
- row_context: bfloat16 [4, 64, 8192], P(None, ('group', 'seq'), 'tp')
All inputs are finite; a program needn't handle non-finite values.
Results may differ from a plain program's by a relative error of at most 0.03.
Values may be sent and summed in bfloat16 or wider, within the bound.
No kernel may reach another device: no remote copies, remote signals or barrier semaphores. Data moves between devices by JAX's collectives and lax.ppermute only.
A program may use at most 64 MiB of HBM per device.

v0:
```python
import jax
import jax.numpy as jnp
import numpy as np
from jax import lax
from jax.sharding import PartitionSpec as P

D = 8192
QH = 64
KVH = 8
HS = 128
TOK_DEV = 384
STEPS = 4


ROPE_BASE = 500000.0
NORM_EPS = 1e-05
NEG_BIG = -1e30


def merged_2(array, axis, combine):
    everything = jax.tree.map(lambda part: lax.all_gather(part, axis), array)
    first = jax.tree.map(lambda part: part[0], everything)

    def lap(k, so_far):
        return combine(so_far, jax.tree.map(lambda part: part[k], everything))

    return lax.fori_loop(1, lax.axis_size(axis), lap, first)


def rotate(values, positions):
    half_dim = values.shape[-1] // 2
    inv_freq = ROPE_BASE ** (-(jnp.arange(half_dim, dtype=jnp.float32) * 2.0 / values.shape[-1]))
    angles = positions.astype(jnp.float32)[:, None] * inv_freq[None, :]
    cosine = jnp.cos(angles)[:, None, :]
    sine_table = jnp.sin(angles)[:, None, :]
    lower_half = values[..., :half_dim]
    upper_half = values[..., half_dim:]
    return jnp.concatenate(
        [
            lower_half * cosine - upper_half * sine_table,
            upper_half * cosine + lower_half * sine_table,
        ],
        axis=-1,
    )


def merge_pair(former, latter):
    highest = jnp.maximum(former[0], latter[0])
    former_scale = jnp.exp(former[0] - highest)
    latter_scale = jnp.exp(latter[0] - highest)
    return (
        highest,
        former[1] * former_scale + latter[1] * latter_scale,
        former[2] * former_scale[..., None] + latter[2] * latter_scale[..., None],
    )


def softmax_state(query_grid, key_rows, value_rows, usable):
    scores = jnp.einsum(
        "srkgh,rnkh->srkgn", query_grid, key_rows, preferred_element_type=jnp.float32
    )
    scores = scores * query_grid.shape[-1] ** (-0.5)
    allowed = usable[:, :, None, None, :]
    highest = jnp.max(jnp.where(allowed, scores, NEG_BIG), axis=-1)
    exp_scores = jnp.where(allowed, jnp.exp(scores - highest[..., None]), 0.0)
    totals = jnp.sum(exp_scores, axis=-1)
    weights = exp_scores.astype(jnp.bfloat16)
    weighted = jnp.einsum(
        "srkgn,rnkh->srkgh", weights, value_rows, preferred_element_type=jnp.float32
    )
    return (highest, totals, weighted)


def passage_reader(everyone, passage_count, query_grid, passage_of_row):
    length = everyone.shape[0] // passage_count
    stacked = everyone.reshape(passage_count, length, 2, KVH, HS)
    picked = jnp.take(stacked, passage_of_row, axis=0)
    usable = jnp.ones((1, picked.shape[0], length), dtype=bool)
    return softmax_state(query_grid, picked[:, :, 0], picked[:, :, 1], usable)


def per_device(
    hidden,
    passage_queries,
    key_weight,
    value_weight,
    decode_queries,
    new_keys,
    new_values,
    cache_keys,
    cache_values,
    cache_lengths,
    passage_of_row,
):
    tp_count = lax.axis_size("tp")
    tp_index = lax.axis_index("tp")
    seq_index = lax.axis_index("seq")
    heads_dev = QH // tp_count
    group_size = QH // KVH
    kv_dev = max(1, KVH // tp_count)
    per_kv = heads_dev // kv_dev
    part_rows = TOK_DEV // tp_count
    scale_factor = HS ** (-0.5)
    widened = hidden[0].astype(jnp.float32)
    squares = lax.psum(jnp.sum(widened * widened, axis=1), "tp")
    inverse = lax.rsqrt(squares / D + NORM_EPS)
    normed = (widened * inverse[:, None]).astype(jnp.bfloat16)
    key_part = jnp.dot(normed, key_weight, preferred_element_type=jnp.float32)
    value_part = jnp.dot(normed, value_weight, preferred_element_type=jnp.float32)
    kv_share = lax.psum_scatter(
        jnp.concatenate([key_part, value_part], axis=1), "tp", scatter_dimension=0, tiled=True
    )
    share_pos = seq_index * TOK_DEV + tp_index * part_rows + jnp.arange(part_rows, dtype=jnp.int32)
    key_share = rotate(kv_share[:, : KVH * HS].reshape(part_rows, KVH, HS), share_pos).astype(
        jnp.bfloat16
    )
    value_share = kv_share[:, KVH * HS :].reshape(part_rows, KVH, HS).astype(jnp.bfloat16)
    kv_pairs = jnp.stack([key_share, value_share], axis=1)
    head_table = (
        (np.arange(tp_count)[:, None] * heads_dev // group_size + np.arange(kv_dev)[None, :])
        .reshape(-1)
        .astype(np.int32)
    )
    pieces = jnp.take(kv_pairs, head_table, axis=2)
    received = lax.all_to_all(pieces, "tp", split_axis=2, concat_axis=0, tiled=True)
    local_kv = received.reshape(TOK_DEV, 2, kv_dev * HS)
    query_pos = seq_index * TOK_DEV + jnp.arange(TOK_DEV, dtype=jnp.int32)
    turned = rotate(
        passage_queries[0].astype(jnp.float32).reshape(TOK_DEV, heads_dev, HS), query_pos
    )
    turned = turned.astype(jnp.bfloat16).reshape(TOK_DEV, kv_dev, per_kv, HS)

    def attend_block(running, element):
        first_pos, key_block = element
        span_rows = key_block.shape[0]
        key_rows = key_block[:, 0].reshape(span_rows, kv_dev, HS)
        value_rows = key_block[:, 1].reshape(span_rows, kv_dev, HS)
        scores = (
            jnp.einsum("qkph,nkh->qkpn", turned, key_rows, preferred_element_type=jnp.float32)
            * scale_factor
        )
        key_pos = first_pos + jnp.arange(span_rows, dtype=jnp.int32)
        allowed = (key_pos[None, :] <= query_pos[:, None])[:, None, None, :]
        highest = jnp.maximum(running[0], jnp.max(jnp.where(allowed, scores, NEG_BIG), axis=-1))
        exp_scores = jnp.where(allowed, jnp.exp(scores - highest[..., None]), 0.0)
        factor = jnp.exp(running[0] - highest)
        totals = running[1] * factor + jnp.sum(exp_scores, axis=-1)
        weighted = running[2] * factor[..., None] + jnp.einsum(
            "qkpn,nkh->qkph",
            exp_scores.astype(jnp.bfloat16),
            value_rows,
            preferred_element_type=jnp.float32,
        )
        return ((highest, totals, weighted), None)

    initial = (
        jnp.full((TOK_DEV, kv_dev, per_kv), NEG_BIG, jnp.float32),
        jnp.zeros((TOK_DEV, kv_dev, per_kv), jnp.float32),
        jnp.zeros((TOK_DEV, kv_dev, per_kv, HS), jnp.float32),
    )
    running = initial
    shard_rows = lax.all_gather(local_kv, "seq", axis=0, tiled=True)
    length = shard_rows.shape[0]
    span_rows = length
    while span_rows > 1024 and span_rows % 2 == 0:
        span_rows = span_rows // 2
    blocks = shard_rows.reshape(length // span_rows, span_rows, 2, kv_dev * HS)
    firsts = span_rows * jnp.arange(length // span_rows, dtype=jnp.int32)
    running, unused = lax.scan(attend_block, running, (firsts, blocks))
    passage_out = (
        (running[2] / running[1][..., None])
        .reshape(TOK_DEV, heads_dev * HS)
        .astype(jnp.bfloat16)[None]
    )
    rows_dev = decode_queries.shape[1]
    passage_count = lax.axis_size("group")
    query_grid = decode_queries.reshape(STEPS, rows_dev, KVH, group_size, HS)
    handed = kv_pairs.reshape(part_rows, 2, KVH * HS)
    everyone = lax.all_gather(handed, ("group", "seq"), axis=0, tiled=True)
    passage_state = passage_reader(everyone, passage_count, query_grid, passage_of_row)
    cache_part = cache_keys.shape[1]
    cache_pos = tp_index * cache_part + jnp.arange(cache_part, dtype=jnp.int32)
    cache_usable = (cache_pos[None, :] < cache_lengths[:, None])[None]
    cache_state = softmax_state(
        query_grid,
        cache_keys.reshape(rows_dev, cache_part, KVH, HS),
        cache_values.reshape(rows_dev, cache_part, KVH, HS),
        cache_usable,
    )
    joined_state = merge_pair(passage_state, cache_state)
    joined_state = (
        joined_state[0].reshape(STEPS, rows_dev, QH),
        joined_state[1].reshape(STEPS, rows_dev, QH),
        joined_state[2].reshape(STEPS, rows_dev, QH, HS),
    )
    merged = merged_2(joined_state, "tp", merge_pair)
    own_state = (
        lax.dynamic_slice_in_dim(merged[0], tp_index * heads_dev, heads_dev, 2),
        lax.dynamic_slice_in_dim(merged[1], tp_index * heads_dev, heads_dev, 2),
        lax.dynamic_slice_in_dim(merged[2], tp_index * heads_dev, heads_dev, 2),
    )
    own_heads = tp_index * heads_dev + jnp.arange(heads_dev, dtype=jnp.int32)
    kv_heads = own_heads // group_size
    own_queries = lax.dynamic_slice_in_dim(
        decode_queries, tp_index * heads_dev * HS, heads_dev * HS, 2
    ).reshape(STEPS, rows_dev, heads_dev, HS)
    recent_keys = jnp.take(new_keys.reshape(STEPS, rows_dev, KVH, HS), kv_heads, axis=2)
    recent_values = jnp.take(new_values.reshape(STEPS, rows_dev, KVH, HS), kv_heads, axis=2)
    recent_scores = (
        jnp.einsum("srah,trah->srat", own_queries, recent_keys, preferred_element_type=jnp.float32)
        * scale_factor
    )
    step_ids = jnp.arange(STEPS, dtype=jnp.int32)
    recent_allowed = (step_ids[None, :] <= step_ids[:, None])[:, None, None, :]
    recent_high = jnp.max(jnp.where(recent_allowed, recent_scores, NEG_BIG), axis=-1)
    recent_exp = jnp.where(recent_allowed, jnp.exp(recent_scores - recent_high[..., None]), 0.0)
    recent_state = (
        recent_high,
        jnp.sum(recent_exp, axis=-1),
        jnp.einsum(
            "srat,trah->srah",
            recent_exp.astype(jnp.bfloat16),
            recent_values,
            preferred_element_type=jnp.float32,
        ),
    )
    final_state = merge_pair(own_state, recent_state)
    row_out = (
        (final_state[2] / final_state[1][..., None])
        .reshape(STEPS, rows_dev, heads_dev * HS)
        .astype(jnp.bfloat16)
    )
    return (passage_out, row_out)


def solution(mesh):
    in_specs = (
        P("group", "seq", "tp"),
        P("group", "seq", "tp"),
        P("tp", None),
        P("tp", None),
        P(None, ("group", "seq"), None),
        P(None, ("group", "seq"), None),
        P(None, ("group", "seq"), None),
        P(("group", "seq"), "tp", None),
        P(("group", "seq"), "tp", None),
        P(("group", "seq")),
        P(("group", "seq")),
    )
    out_specs = (P("group", "seq", "tp"), P(None, ("group", "seq"), "tp"))
    return jax.shard_map(
        per_device, mesh=mesh, in_specs=in_specs, out_specs=out_specs, check_vma=False
    )
```

profile of v0, /device:TPU:1, one launch (start us, length us, event | category | flops | bytes accessed | tf_op | source)
XLA Modules:
  0.0 410.2 jit_solution(11734370631247869040)
XLA Ops:
  7.2 1.3 fusion.36
  8.6 29.8 %psum.7 = f32[384]{0:T(512)S(1)} all-reduce(f32[384]{0:T(512)S(1)} %fusion.36), channel_id=1, replica_groups=mesh['group'=4,'seq'=8,'tp'=16] {'tp'}, use_global_device_ids=true, to_apply=%region_1.0 | all-reduce | flops 384 | bytes 3072 | tf_op jit(solution)/shard_map/psum | solution.py:105
  38.3 1.6 fusion.48
  40.6 2.0 pad_maximum_fusion
  42.9 60.6 %reduce-scatter.2.cloned.1.call-done = f32[24,2048]{1,0:T(8,128)} async-done(((f32[384,2048]{1,0:T(8,128)}), f32[24,2048]{1,0:T(8,128)}) %reduce-scatter.2.cloned.1.call-update) | async-done | bytes 196624 | tf_op jit(solution)/shard_map/reduce_scatter | solution.py:110
  109.7 1.3 gather_fusion
  110.9 7.1 %all-to-all-start = ((bf16[24,2,16,128]{3,0,1,2:T(8,128)(2,1)}), bf16[24,2,16,128]{3,0,1,2:T(8,128)(2,1)S(1)}, u32[]{:S(2)}, u32[]{:S(2)}) async-start(bf16[24,2,16,128]{3,0,1,2:T(8,128)(2,1)} %bitcast.7), calls=%async_computation.1 | async-start | bytes 393216 | tf_op jit(solution)/shard_map/all_to_all | solution.py:125
  122.2 6.1 %all-to-all-done = bf16[24,2,16,128]{3,0,1,2:T(8,128)(2,1)S(1)} async-done(((bf16[24,2,16,128]{3,0,1,2:T(8,128)(2,1)}), bf16[24,2,16,128]{3,0,1,2:T(8,128)(2,1)S(1)}, u32[]{:S(2)}, u32[]{:S(2)}) %all-to-all-start) | async-done | bytes 196640 | tf_op jit(solution)/shard_map/all_to_all | solution.py:125
  132.4 106.0 %all-gather.6.cloned.1.call-done = bf16[768,2,1024]{2,0,1:T(8,128)(2,1)} async-done(((bf16[24,2,1024]{2,0,1:T(8,128)(2,1)}), bf16[768,2,1024]{2,0,1:T(8,128)(2,1)}) %all-gather.6.cloned.1.call-update) | async-done | bytes 3145744 | tf_op jit(solution)/shard_map/all_gather | solution.py:179
  238.4 2.7 copy.184
  241.1 2.2 copy.136
  243.3 2.7 gather_fusion.1
  249.1 53.9 %all-gather.4.cloned.1.call-done = bf16[3072,2,128]{2,0,1:T(8,128)(2,1)} async-done(((bf16[384,2,128]{2,0,1:T(8,128)(2,1)}), bf16[3072,2,128]{2,0,1:T(8,128)(2,1)}) %all-gather.4.cloned.1.call-update) | async-done | bytes 1572880 | tf_op jit(solution)/shard_map/all_gather | solution.py:162
  303.1 42.4 %while.35 = (s32[]{:T(128)}, f32[384,1,4]{0,2,1:T(4,128)S(1)}, f32[384,1,4]{0,2,1:T(4,128)S(1)}, f32[384,1,4,128]{0,3,2,1:T(8,128)S(1)}, s32[4]{0:T(128)S(1)}, /...) while((s32[]{:T(128)}, f32[384,1,4]{0,2,1:T(4,128)S(1)}, ...), condition=%wide.region_6.7_spmd.clone, body=%wide.region_3.6_spmd.clone.sunk | while | flops 617851008 | bytes 37463388 | solution.py:169
  305.6 3.1 fusion.94
  308.7 3.8 fusion.97
  316.1 3.1 fusion.94
  319.2 3.9 fusion.97
  326.8 3.1 fusion.94
  329.8 3.9 fusion.97
  337.4 3.1 fusion.94
  340.5 3.9 fusion.97
  347.0 19.8 %all_gather.17 = f32[16,4,2,64]{3,1,2,0:T(4,128)S(1)} all-gather(f32[1,4,2,64]{3,1,2,0:T(4,128)S(1)} %copy.143), channel_id=1, replica_groups=mesh['group'=4,'seq'=8,'tp'=16] {'tp'}, dimensions={0}, use_global_device_ids=true | all-gather | bytes 34816 | tf_op jit(solution)/shard_map/all_gather | solution.py:21
  366.8 15.4 %all_gather.18 = f32[16,4,2,64]{3,1,2,0:T(4,128)S(1)} all-gather(f32[1,4,2,64]{3,1,2,0:T(4,128)S(1)} %copy.146), channel_id=1, replica_groups=mesh['group'=4,'seq'=8,'tp'=16] {'tp'}, dimensions={0}, use_global_device_ids=true | all-gather | bytes 34816 | tf_op jit(solution)/shard_map/all_gather | solution.py:21
  383.1 19.2 %while.34 = (s32[]{:T(128)}, f32[4,2,64]{2,1,0:T(2,128)S(1)}, f32[4,2,64]{2,1,0:T(2,128)S(1)}, f32[4,2,64,128]{3,2,1,0:T(8,128)S(1)}, f32[16,4,2,64]{3,1,2,0:T(4...) while((s32[]{:T(128)}, f32[4,2,64]{2,1,0:T(2,128)S(1)}, ...), condition=%wide.region_12.13_spmd, body=%wide.region_11.12_spmd.sunk | while | flops 199685 | bytes 815255 | solution.py:27
  383.2 1.2 fusion.92
  384.5 1.2 fusion.92
  385.8 1.2 fusion.92
  388.3 1.2 fusion.92
  389.6 1.2 fusion.92
  390.9 1.2 fusion.92
  392.2 1.2 fusion.92
  (243 shorter events, 46.2 us)
Async XLA Ops:
  7.2 31.2 %copy-start = (bf16[512,1024]{1,0:T(8,128)(2,1)S(1)}, bf16[512,1024]{1,0:T(8,128)(2,1)}, u32[]{:S(2)}) copy-start(bf16[512,1024]{1,0:T(8,128)(2,1)} %param.21) | copy-start | bytes 3145732
  7.2 32.8 %copy-start.2 = (bf16[1,384,512]{2,1,0:T(8,128)(2,1)S(1)}, bf16[1,384,512]{2,1,0:T(8,128)(2,1)}, u32[]{:S(2)}) copy-start(bf16[1,384,512]{2,1,0:T(8,128)(2,1)} %param.18) | copy-start | bytes 1179652
  7.2 32.8 %copy-start.3 = (bf16[512,1024]{1,0:T(8,128)(2,1)S(1)}, bf16[512,1024]{1,0:T(8,128)(2,1)}, u32[]{:S(2)}) copy-start(bf16[512,1024]{1,0:T(8,128)(2,1)} %param.20) | copy-start | bytes 3145732
  7.2 96.3 %reduce-scatter.2.cloned.1.call-start = ((), (), s32[]{:S(2)}) async-start(), calls=%async_computation.2 | async-start | bytes 3342336 | tf_op jit(solution)/shard_map/reduce_scatter | solution.py:110
  42.6 63.6 %copy-start.12 = (bf16[4,2,8192]{2,1,0:T(2,128)(2,1)S(1)}, bf16[4,2,8192]{2,1,0:T(2,128)(2,1)}, u32[]{:S(2)}) copy-start(bf16[4,2,8192]{2,1,0:T(2,128)(2,1)} %param.22) | copy-start | bytes 393220
  42.6 63.7 %copy-start.7 = (bf16[2,128,1024]{2,1,0:T(8,128)(2,1)S(1)}, bf16[2,128,1024]{2,1,0:T(8,128)(2,1)}, u32[]{:S(2)}) copy-start(bf16[2,128,1024]{2,1,0:T(8,128)(2,1)} %param.25) | copy-start | bytes 1572868
  42.6 63.8 %copy-start.9 = (bf16[1,384,512]{2,1,0:T(8,128)(2,1)S(1)}, bf16[1,384,512]{2,1,0:T(8,128)(2,1)}, u32[]{:S(2)}) copy-start(bf16[1,384,512]{2,1,0:T(8,128)(2,1)} %param.19) | copy-start | bytes 1179652
  42.6 64.7 %copy-start.22 = (s32[16]{0:T(128)S(1)}, s32[16]{0:T(128)}, u32[]{:S(2)}) copy-start(s32[16]{0:T(128)} %constant.175) | copy-start | bytes 196
  42.7 65.4 %copy-start.24 = (s32[2]{0:T(128)S(1)}, s32[2]{0:T(128)}, u32[]{:S(2)}) copy-start(s32[2]{0:T(128)} %param.27) | copy-start | bytes 28
  42.7 195.7 %all-gather.6.cloned.1.call-start = ((), (), s32[]{:S(2)}) async-start(), calls=%async_computation.4 | async-start | bytes 3244032 | tf_op jit(solution)/shard_map/all_gather | solution.py:179
  106.3 3.0 copy-start.5
  108.1 1.3 copy-start.18
  108.1 12.6 %copy-start.13 = (bf16[4,2,1024]{2,1,0:T(2,128)(2,1)S(1)}, bf16[4,2,1024]{2,1,0:T(2,128)(2,1)}, u32[]{:S(2)}) copy-start(bf16[4,2,1024]{2,1,0:T(2,128)(2,1)} %param.23) | copy-start | bytes 49156
  108.1 10.0 %copy-start.23 = (s32[4]{0:T(128)S(1)}, s32[4]{0:T(128)}, u32[]{:S(2)}) copy-start(s32[4]{0:T(128)} %compare_select_fusion) | copy-start | bytes 52
  108.1 12.5 %copy-start.14 = (bf16[4,2,1024]{2,1,0:T(2,128)(2,1)S(1)}, bf16[4,2,1024]{2,1,0:T(2,128)(2,1)}, u32[]{:S(2)}) copy-start(bf16[4,2,1024]{2,1,0:T(2,128)(2,1)} %param.24) | copy-start | bytes 49156
  108.6 20.4 %copy-start.10 = (f32[4,2,8,8,128]{4,3,0,2,1:T(8,128)}, f32[4,2,8,8,128]{4,3,0,2,1:T(8,128)S(1)}, u32[]{:S(2)}) copy-start(f32[4,2,8,8,128]{4,3,0,2,1:T(8,128)S(1)} %get-tuple-element.367) | copy-start | bytes 786436
  110.9 17.5 %all-to-all-start = ((bf16[24,2,16,128]{3,0,1,2:T(8,128)(2,1)}), bf16[24,2,16,128]{3,0,1,2:T(8,128)(2,1)S(1)}, u32[]{:S(2)}, u32[]{:S(2)}) async-start(bf16[24,2,16,128]{3,0,1,2:T(8,128)(2,1)} %bitcast.7), calls=%async_computation.1 | async-start | bytes 393216 | tf_op jit(solution)/shard_map/all_to_all | solution.py:125
  118.0 185.0 %all-gather.4.cloned.1.call-start = ((), (), s32[]{:S(2)}) async-start(), calls=%async_computation.3 | async-start | bytes 1769472 | tf_op jit(solution)/shard_map/all_gather | solution.py:162
  122.2 118.9 %copy-start.20 = (pred[4,4]{0,1:T(4,128)(4,1)}, pred[4,4]{0,1:T(4,128)(4,1)S(1)}, u32[]{:S(2)}) copy-start(pred[4,4]{0,1:T(4,128)(4,1)S(1)} %iota_compare_fusion) | copy-start | bytes 52
  129.1 253.1 %all-gather.8.cloned.1.call-start = ((), (), s32[]{:S(2)}) async-start(), calls=%async_computation.5 | async-start | bytes 4456448 | tf_op jit(solution)/shard_map/all_gather | solution.py:21
  246.0 2.0 copy-start.8
  246.0 2.0 copy-start.11
  246.0 2.0 copy-start.19
  246.9 56.2 %copy-start.4 = (f32[384,1,4,128]{0,3,2,1:T(8,128)S(1)}, f32[384,1,4,128]{0,3,2,1:T(8,128)}, u32[]{:S(2)}) copy-start(f32[384,1,4,128]{0,3,2,1:T(8,128)} %custom-call.2) | copy-start | bytes 2359300
  303.1 43.9 %copy-start.15 = (f32[1,4,2,64]{3,2,1,0:T(2,128)S(1)}, f32[1,4,2,64]{3,2,1,0:T(2,128)}, u32[]{:S(2)}) copy-start(f32[1,4,2,64]{3,2,1,0:T(2,128)} %reduce_sum.55) | copy-start | bytes 6148
  303.1 43.9 %copy-start.16 = (f32[1,4,2,64]{3,2,1,0:T(2,128)S(1)}, f32[1,4,2,64]{3,2,1,0:T(2,128)}, u32[]{:S(2)}) copy-start(f32[1,4,2,64]{3,2,1,0:T(2,128)} %reduce_max.45) | copy-start | bytes 6148
  308.7 3.8 copy-start.1
  319.2 4.0 copy-start.1
  329.8 3.9 copy-start.1
  340.4 3.9 copy-start.1
  346.7 56.0 %copy-start.17 = (bf16[4,2,4,128]{3,0,1,2:T(4,128)(2,1)S(1)}, bf16[4,2,4,128]{3,0,1,2:T(4,128)(2,1)}, u32[]{:S(2)}) copy-start(bf16[4,2,4,128]{3,0,1,2:T(4,128)(2,1)} %get-tuple-element.364) | copy-start | bytes 24580
  346.7 56.0 %copy-start.21 = (pred[4,4]{0,1:T(4,128)(4,1)S(1)}, pred[4,4]{0,1:T(4,128)(4,1)}, u32[]{:S(2)}) copy-start(pred[4,4]{0,1:T(4,128)(4,1)} %copy-done.20) | copy-start | bytes 52
  (9 other events, 10.2 us)
Sparse Core Ops, SparseCore 0:
  42.8 60.6 reduce-scatter.1
  106.3 131.9 all-gather.5
  240.5 62.5 all-gather.3
  305.0 46.0 all-gather.7
where the time goes:
time: 411 us; the launch traced here: 410 us
  waiting for transfers between devices  227 us (55%)
  blocking collectives  64.9 us (16%)
  other arithmetic  35.1 us (9%)
  matrix products  32.1 us (8%)
  local copies, waits for them, and re-layouts  28.6 us (7%)
  between operations  14.4 us (4%)
  starting transfers between devices  7.47 us (2%)
    all_gather x1, waiting for transfers between devices, per_device(): everyone = lax.all_gather(handed, ('group', 'seq'), axis=0, tiled=True)  106 us
    reduce_scatter x1, waiting for transfers between devices, per_device(): lax.psum_scatter(jnp.concatenate([key_part, value_part], axis=1), 'tp', s...  60.6 us
    all_gather x1, waiting for transfers between devices, per_device(): shard_rows = lax.all_gather(local_kv, 'seq', axis=0, tiled=True)  53.9 us
    all_gather x2, blocking collectives, merged_2(): everything = jax.tree.map(lambda part: lax.all_gather(part, axis), array)  35.1 us
    psum x1, blocking collectives, per_device(): squares = lax.psum(jnp.sum(widened * widened, axis=1), 'tp')  29.8 us
    add x15, other arithmetic, merge_pair(): former[2] * former_scale[..., None] + latter[2] * latter_scale[..., None]  18.2 us
    dot_general x4, matrix products, attend_block(): jnp.einsum('qkpn,nkh->qkph', exp_scores.astype(jnp.bfloat16), value_rows,...  15.4 us
    dot_general x4, matrix products, attend_block(): jnp.einsum('qkph,nkh->qkpn', turned, key_rows, preferred_element_type=jnp...  12.2 us
  transfers between devices with their start and end apart: 5, of which 4 were waited for; matrix products, arithmetic and copies ran while one was open for 16% of the time, Pallas kernels for 0%

commit v1 on v0

v1 whole, which is shorter than its diff:
```python
import functools

import jax
import jax.numpy as jnp
import numpy as np
from jax import lax
from jax.experimental import pallas as pl
from jax.experimental.pallas import tpu as pltpu
from jax.sharding import Mesh
from jax.sharding import PartitionSpec as P

D = 8192
KVH = 8
HS = 128
SEQ = 8
TOK = 384
HALF = 192
HEADS = 4
EXTRA = 16
STATE = 40
ROPE_BASE = 500000.0
NORM_EPS = 1e-05
NEG = -1e30
SCALE2 = float(HS**-0.5 * np.log2(np.e))

bf16, f32 = jnp.bfloat16, jnp.float32
dot = functools.partial(jnp.dot, preferred_element_type=f32)


def dot_t(a, b):
    return lax.dot_general(a, b, (((1,), (1,)), ((), ())), preferred_element_type=f32)


def tables():
    freq = ROPE_BASE ** (-(np.arange(HS // 2) * 2.0 / HS))
    freq = np.concatenate([freq, freq])
    near = np.arange(TOK)[:, None] * freq
    far = (np.arange(SEQ) * TOK)[:, None] * freq
    near = np.stack([np.cos(near), np.sin(near)]).astype(np.float32)
    far = np.stack([np.cos(far), np.sin(far)]).astype(np.float32)
    return near, far


def turn_by(near_ref, far_ref, s, rows):
    cn, sn = near_ref[0, rows, :], near_ref[1, rows, :]
    cf, sf = far_ref[0, pl.ds(s, 1), :], far_ref[1, pl.ds(s, 1), :]
    cosine = cn * cf - sn * sf
    sine = sn * cf + cn * sf
    lane = lax.broadcasted_iota(jnp.int32, sine.shape, 1)
    return cosine, jnp.where(lane < HS // 2, -sine, sine)


def turned(x, cosine, sine):
    return x * cosine + pltpu.roll(x, HS // 2, 1) * sine


def project(mine, where_ref, hidden_ref, key_ref, value_ref, out_ref, squares_ref):
    core = where_ref[1] if mine else 1 - where_ref[1]
    rows = pl.ds(pl.multiple_of(core * HALF, HALF), HALF)

    @pl.when(pl.program_id(0) == 0)
    def _():
        h = hidden_ref[rows, :].astype(f32)
        sq = h * h
        high = sq.astype(bf16)
        low = (sq - high.astype(f32)).astype(bf16)
        ones = jnp.ones((EXTRA, hidden_ref.shape[1]), bf16)
        sums = dot_t(ones, high) + dot_t(ones, low)
        sums = jnp.concatenate([sums, jnp.zeros((EXTRA, 256 - HALF), f32)], axis=1)
        row = lax.broadcasted_iota(jnp.int32, (EXTRA, 256), 0)
        squares_ref[...] = jnp.where(row == where_ref[2], sums, 0.0).astype(bf16)

    h = hidden_ref[rows, :]
    keys = dot(h, key_ref[...]).astype(bf16)
    values = dot(h, value_ref[...]).astype(bf16)
    for j in range(out_ref.shape[0]):
        out_ref[j, :HALF, :HS] = keys[:, j * HS : (j + 1) * HS]
        out_ref[j, :HALF, HS:] = values[:, j * HS : (j + 1) * HS]
        out_ref[j, HALF:, :] = squares_ref[...]


def add(mine_ref, other_ref, out_ref):
    out_ref[...] = (mine_ref[...].astype(f32) + other_ref[...].astype(f32)).astype(bf16)


def finish_share(where_ref, sums_ref, near_ref, far_ref, out_ref):
    s, core = where_ref[0], where_ref[1]
    squares, sums = 0.0, 0.0
    for k in range(sums_ref.shape[0]):
        sums = sums + sums_ref[k, :HALF, :].astype(f32)
        squares = squares + sums_ref[k, HALF:, :].astype(f32)
    squares = jnp.sum(squares, axis=0, keepdims=True)
    inverse = lax.rsqrt(squares * (1.0 / D) + NORM_EPS)
    inverse = jnp.transpose(jnp.broadcast_to(inverse, (8, 256)))[:HALF, 0:1]
    alive = inverse > 0.0
    scaled = jnp.where(alive, sums * inverse, 0.0)
    rows = pl.ds(pl.multiple_of(core * HALF, HALF), HALF)
    cosine, sine = turn_by(near_ref, far_ref, s, rows)
    keys = turned(scaled[:, :HS], cosine, sine)
    share = jnp.concatenate([keys, scaled[:, HS:]], axis=1).astype(bf16)
    for to in range(SEQ):
        out_ref[to] = share


def put_state(out_ref, at, weighted, highest, totals):
    rows = weighted.shape[0]
    lane = lax.broadcasted_iota(jnp.int32, (rows, HS), 1)
    both = jnp.where(lane == 0, highest, jnp.where(lane == 1, totals, 0.0))
    flat = jnp.transpose(both)[:8, :]
    for j in range(rows // 32):
        out_ref[at + j, :32, :] = weighted[j * 32 : (j + 1) * 32, :]
        out_ref[at + j, 32:, :] = jnp.concatenate(
            [flat[:, j * 32 : (j + 1) * 32], jnp.zeros((8, HS - 32), f32)], axis=1
        )


def cache_states(
    where_ref, length_ref, query_ref, new_ref, key_ref, value_ref, out_ref
):
    tp = where_ref[2]
    slots = key_ref.shape[1]
    rows = 64
    q = lax.broadcasted_iota(jnp.int32, (rows, 2 * slots), 0)
    n = lax.broadcasted_iota(jnp.int32, (rows, 2 * slots), 1)
    key_row = jnp.where(n >= slots, 1, 0)
    slot = tp * slots + n - key_row * slots
    length = jnp.where(key_row == 1, length_ref[1], length_ref[0])
    live = ((q & 1) == key_row) & (slot < length)
    q = lax.broadcasted_iota(jnp.int32, (rows, 8), 0)
    n = lax.broadcasted_iota(jnp.int32, (rows, 8), 1)
    recent = ((q & 1) == (n & 1)) & ((n & 7) >> 1 <= (q & 7) >> 1) & (tp == 0)
    for head in range(KVH):
        cols = slice(head * HS, (head + 1) * HS)
        query = jnp.concatenate(
            [query_ref[:, (head * 8 + p) * HS : (head * 8 + p + 1) * HS] for p in range(8)], axis=0
        )
        low = query.astype(bf16)
        keys = jnp.concatenate([key_ref[0, :, cols], key_ref[1, :, cols]], axis=0)
        values = jnp.concatenate([value_ref[0, :, cols], value_ref[1, :, cols]], axis=0)
        new_keys = new_ref[:, cols].astype(bf16)
        new_values = new_ref[:, KVH * HS + head * HS : KVH * HS + (head + 1) * HS].astype(bf16)
        scores = jnp.where(live, dot_t(low, keys) * SCALE2, NEG)
        news = jnp.where(recent, dot_t(low, new_keys) * SCALE2, NEG)
        highest = jnp.maximum(
            jnp.max(scores, axis=1, keepdims=True), jnp.max(news, axis=1, keepdims=True)
        )
        weights = jnp.where(live, jnp.exp2(scores - highest), 0.0)
        new_weights = jnp.where(recent, jnp.exp2(news - highest), 0.0)
        totals = jnp.sum(weights, axis=1, keepdims=True) + jnp.sum(
            new_weights, axis=1, keepdims=True
        )
        weighted = dot(weights.astype(bf16), values) + dot(new_weights.astype(bf16), new_values)
        put_state(out_ref, 2 * head, weighted, highest, totals)


def passage_states(query_ref, own_ref, other_ref, out_ref):
    query = jnp.concatenate(
        [
            query_ref[g, :, p * HS : (p + 1) * HS]
            for g in range(query_ref.shape[0])
            for p in range(HEADS)
        ],
        axis=0,
    ).astype(bf16)
    refs = (own_ref, other_ref)
    scores = [dot_t(query, ref[:, :HS]) * SCALE2 for ref in refs]
    highest = jnp.max(jnp.maximum(*scores), axis=1, keepdims=True)
    weights = [jnp.exp2(score - highest) for score in scores]
    totals = jnp.sum(weights[0] + weights[1], axis=1, keepdims=True)
    weighted = sum(dot(w.astype(bf16), ref[:, HS:]) for w, ref in zip(weights, refs, strict=True))
    put_state(out_ref, 0, weighted, highest, totals)


def attend(
    where_ref,
    query_ref,
    near_ref,
    far_ref,
    own_ref,
    other_ref,
    out_ref,
    high_ref,
    sum_ref,
    turned_ref,
):
    s, core = where_ref[0], where_ref[1]
    cosine, sine = turn_by(near_ref, far_ref, s, slice(None))
    for h in range(HEADS):
        x = query_ref[:, h * HS : (h + 1) * HS].astype(f32)
        turned_ref[h] = turned(x, cosine, sine).astype(bf16)
    ones = jnp.ones((TOK, HS), bf16)
    last = s // 2

    def blocks(pair):
        at = pl.multiple_of(pair * TOK, TOK)
        return [ref[pl.ds(at, TOK), :] for ref in (own_ref, other_ref)]

    def weigh(scores, highest, kv):
        total = 0.0
        for score, block in zip(scores, kv, strict=True):
            weights = jnp.exp2(score * SCALE2 - highest * SCALE2).astype(bf16)
            total = total + dot(weights, jnp.concatenate([block[:, HS:], ones], axis=1))
        return total

    kv = blocks(last)
    query_pos = s * TOK + lax.broadcasted_iota(jnp.int32, (TOK, TOK), 0)
    n = lax.broadcasted_iota(jnp.int32, (TOK, TOK), 1)
    second = jnp.where(n >= HALF, 1, 0)
    key_pos = (2 * last + second) * TOK + n - second * HALF
    allowed = [key_pos + c * HALF <= query_pos for c in (core, 1 - core)]
    for h in range(HEADS):
        query = turned_ref[h]
        scores = [
            jnp.where(ok, dot_t(query, block[:, :HS]), NEG)
            for ok, block in zip(allowed, kv, strict=True)
        ]
        highest = jnp.max(jnp.maximum(scores[0], scores[1]), axis=1, keepdims=True)
        high_ref[h] = jnp.broadcast_to(highest, (TOK, HS))
        sum_ref[h] = weigh(scores, highest, kv)

    def step(i, carry):
        kv = blocks(last - 1 - i)
        for h in range(HEADS):
            query = turned_ref[h]
            scores = [dot_t(query, block[:, :HS]) for block in kv]
            before = high_ref[h, :, 0:1]
            highest = jnp.maximum(
                before, jnp.max(jnp.maximum(scores[0], scores[1]), axis=1, keepdims=True)
            )
            factor = jnp.exp2((before - highest) * SCALE2)
            high_ref[h] = jnp.broadcast_to(highest, (TOK, HS))
            sum_ref[h] = sum_ref[h] * factor + weigh(scores, highest, kv)
        return carry

    lax.fori_loop(0, last, step, 0)
    for h in range(HEADS):
        out_ref[:, h * HS : (h + 1) * HS] = (
            sum_ref[h, :, :HS] / sum_ref[h, :, HS : HS + 1]
        ).astype(bf16)


def merge(passage_ref, passages_ref, caches_ref, out_ref):
    count, sources = passages_ref.shape[0], caches_ref.shape[0]
    tail = jnp.transpose(caches_ref[:, 32:, :].reshape(sources * 8, HS))[:32, :]
    row = lax.broadcasted_iota(jnp.int32, (32, 1), 0) & 1
    chosen = jnp.where(row == 1, passage_ref[1], passage_ref[0])
    tails = jnp.concatenate(
        [passages_ref[:, 32:, :].reshape(count * 8, HS), jnp.zeros((HS - count * 8, HS), f32)],
        axis=0,
    )
    tails = jnp.transpose(tails)[:32, :]
    highs = [tail[:, 8 * t : 8 * t + 1] for t in range(sources)]
    totals = [tail[:, 8 * t + 1 : 8 * t + 2] for t in range(sources)]
    states = [caches_ref[t, :32, :] for t in range(sources)]
    high, total, state = tails[:, 0:1], tails[:, 1:2], passages_ref[0, :32, :]
    for g in range(1, count):
        high = jnp.where(chosen == g, tails[:, 8 * g : 8 * g + 1], high)
        total = jnp.where(chosen == g, tails[:, 8 * g + 1 : 8 * g + 2], total)
        state = jnp.where(chosen == g, passages_ref[g, :32, :], state)
    highest = functools.reduce(jnp.maximum, highs, high)
    factor = jnp.exp2(high - highest)
    total, state = total * factor, state * factor
    for t in range(sources):
        factor = jnp.exp2(highs[t] - highest)
        total = total + totals[t] * factor
        state = state + states[t] * factor
    context = state / total
    for p in range(HEADS):
        out_ref[:, p * HS : (p + 1) * HS] = context[p * 8 : (p + 1) * 8, :]


def vmem(count):
    return [pl.BlockSpec(memory_space=pltpu.VMEM)] * count


def smem(count):
    return [pl.BlockSpec(memory_space=pltpu.SMEM)] * count


def params(mib):
    return pltpu.CompilerParams(vmem_limit_bytes=mib << 20)


def cost(flops, transcendentals=0, bytes_accessed=1 << 20):
    return pl.CostEstimate(
        flops=flops, transcendentals=transcendentals, bytes_accessed=bytes_accessed
    )


def per_device(
    hidden,
    passage_queries,
    key_weight,
    value_weight,
    decode_queries,
    new_keys,
    new_values,
    cache_keys,
    cache_values,
    cache_lengths,
    passage_of_row,
):
    near, far = tables()
    core, y, s = lax.axis_index("core"), lax.axis_index("y"), lax.axis_index("seq")
    groups = lax.axis_size("group")
    tp = y * 2 + core
    where = jnp.stack([s, core, tp, tp]).astype(jnp.int32)
    features = hidden.shape[2]

    with jax.named_scope("decode_query_exchange"):
        queries = decode_queries.reshape(8, -1).astype(f32)
        own = lax.dynamic_slice_in_dim(queries, tp * HEADS * HS, HEADS * HS, 1)
        own = jnp.broadcast_to(own[None], (groups, 8, HEADS * HS))
        group_queries = lax.all_to_all(own, "group", 0, 0, tiled=True)

    swap = [(0, 1), (1, 0)]
    with jax.named_scope("projection"):
        width = 2

        def projected(mine):
            return pl.pallas_call(
                functools.partial(project, mine),
                grid=(KVH // width,),
                in_specs=smem(1)
                + [
                    pl.BlockSpec((TOK, features), lambda i: (0, 0)),
                    pl.BlockSpec((features, width * HS), lambda i: (0, i)),
                    pl.BlockSpec((features, width * HS), lambda i: (0, i)),
                ],
                out_specs=pl.BlockSpec((width, HALF + EXTRA, 2 * HS), lambda i: (i, 0, 0)),
                out_shape=jax.ShapeDtypeStruct((KVH, HALF + EXTRA, 2 * HS), bf16),
                scratch_shapes=[pltpu.VMEM((EXTRA, 256), bf16)],
                compiler_params=params(56),
                cost_estimate=cost(TOK * features * 2048, 0, 4 << 20),
            )(where, hidden[0], key_weight, value_weight)

        theirs = lax.ppermute(projected(False), "core", swap)
        chunks = pl.pallas_call(
            add,
            in_specs=vmem(2),
            out_specs=vmem(1)[0],
            out_shape=jax.ShapeDtypeStruct((KVH, HALF + EXTRA, 2 * HS), bf16),
            compiler_params=params(32),
            cost_estimate=cost(1 << 20),
        )(projected(True), theirs)
        sums = lax.all_to_all(chunks, "y", 0, 0, tiled=True)

    with jax.named_scope("share"):
        share = pl.pallas_call(
            finish_share,
            in_specs=smem(1) + vmem(3),
            out_specs=vmem(1)[0],
            out_shape=jax.ShapeDtypeStruct((SEQ, HALF, 2 * HS), bf16),
            compiler_params=params(32),
            cost_estimate=cost(1 << 20),
        )(where, sums, near, far)
        received = lax.all_to_all(share, "seq", 0, 0, tiled=True)

    with jax.named_scope("cache"):
        news = jnp.concatenate([new_keys, new_values], axis=2).reshape(8, -1).astype(f32)
        news, queries, _ = lax.optimization_barrier((news, queries, chunks))
        cached = pl.pallas_call(
            cache_states,
            in_specs=smem(2) + vmem(4),
            out_specs=vmem(1)[0],
            out_shape=jax.ShapeDtypeStruct((16, STATE, HS), f32),
            compiler_params=params(32),
            cost_estimate=cost(8 * 64 * 256 * 128 * 4, 8 * 64 * 256, 2 << 20),
        )(where, cache_lengths, queries, news, cache_keys, cache_values)
        cached, _ = lax.optimization_barrier((cached, share))
        cached = lax.all_to_all(cached, ("y", "core"), 0, 0, tiled=True)

    with jax.named_scope("passage_rows"):
        own_kv = received.reshape(SEQ * HALF, 2 * HS)
        other_kv = lax.ppermute(own_kv, "core", swap)
        rows_passage = pl.pallas_call(
            passage_states,
            in_specs=vmem(3),
            out_specs=vmem(1)[0],
            out_shape=jax.ShapeDtypeStruct((groups, STATE, HS), f32),
            compiler_params=params(32),
            cost_estimate=cost(128 * 3072 * 128 * 4, 128 * 3072, 2 << 20),
        )(group_queries, own_kv, other_kv)
        returned = lax.all_to_all(rows_passage, "group", 0, 0, tiled=True)

    with jax.named_scope("passage_attention"):
        passage_out = pl.pallas_call(
            attend,
            in_specs=smem(1) + vmem(5),
            out_specs=vmem(1)[0],
            out_shape=jax.ShapeDtypeStruct((TOK, HEADS * HS), bf16),
            scratch_shapes=[
                pltpu.VMEM((HEADS, TOK, HS), f32),
                pltpu.VMEM((HEADS, TOK, 2 * HS), f32),
                pltpu.VMEM((HEADS, TOK, HS), bf16),
            ],
            compiler_params=params(48),
            cost_estimate=cost(1536 * 3072 * 128 * 4 * 4, 1536 * 3072, 3 << 20),
        )(where, passage_queries[0], near, far, own_kv, other_kv)

    with jax.named_scope("row_merge"):
        row_out = pl.pallas_call(
            merge,
            in_specs=smem(1) + vmem(2),
            out_specs=vmem(1)[0],
            out_shape=jax.ShapeDtypeStruct((8, HEADS * HS), f32),
            compiler_params=params(32),
            cost_estimate=cost(1 << 20),
        )(passage_of_row, returned, cached)
    return passage_out[None], row_out.astype(bf16).reshape(4, 2, HEADS * HS)


def solution(mesh):
    shape = tuple(mesh.shape[name] for name in ("group", "seq", "tp"))
    split = Mesh(
        mesh.devices.reshape(shape[0], shape[1], shape[2] // 2, 2), ("group", "seq", "y", "core")
    )
    tp, rows = ("y", "core"), ("group", "seq")
    in_specs = (
        P("group", "seq", tp),
        P("group", "seq", tp),
        P(tp, None),
        P(tp, None),
        P(None, rows, None),
        P(None, rows, None),
        P(None, rows, None),
        P(rows, tp, None),
        P(rows, tp, None),
        P(rows),
        P(rows),
    )
    out_specs = (P("group", "seq", tp), P(None, rows, tp))
    return jax.shard_map(
        per_device, mesh=split, in_specs=in_specs, out_specs=out_specs, check_vma=False
    )
```

time: 411 us -> 120 us (0.29)
  waiting for transfers between devices: 227 us -> 26.8 us
  blocking collectives: 64.9 us -> 27.5 us
  other arithmetic: 35.1 us -> 0.7 us
  matrix products: 32.1 us -> 0 us
  starting transfers between devices: 7.47 us -> 37.2 us
  local copies, waits for them, and re-layouts: 28.6 us -> 3.11 us
  Pallas kernels: 0 us -> 21.7 us
  between operations: 14.4 us -> 0.81 us
    all_gather x3 -> x0, waiting for transfers between devices: 160 us -> none  [the longest x1 106 us: per_device(): everyone = lax.all_gather(handed, ('group', 'seq'), axis=0, tiled=True)]
    reduce_scatter x1 -> x0, waiting for transfers between devices: 60.6 us -> none  [per_device(): lax.psum_scatter(jnp.concatenate([key_part, value_part], axis=1), 'tp', s...]
    all_gather x2 -> x0, blocking collectives: 35.1 us -> none  [merged_2(): everything = jax.tree.map(lambda part: lax.all_gather(part, axis), array)]
    dot_general x16 -> x0, matrix products: 32.1 us -> none  [the longest x4 15.4 us: attend_block(): jnp.einsum('qkpn,nkh->qkph', exp_scores.astype(jnp.bfloat16), value_rows,...]
    psum x1 -> x0, blocking collectives: 29.8 us -> none  [per_device(): squares = lax.psum(jnp.sum(widened * widened, axis=1), 'tp')]
    all_to_all x0 -> x1, blocking collectives: none -> 27.5 us  [per_device(): sums = lax.all_to_all(chunks, 'y', 0, 0, tiled=True)]
    pallas_call x0 -> x8, Pallas kernels: none -> 21.7 us  [the longest x2 8.82 us: projected(): pl.pallas_call(functools.partial(project, mine), grid=(KVH // width,), in...]
    add x45 -> x0, other arithmetic: 21.3 us -> none  [the longest x15 18.2 us: merge_pair(): former[2] * former_scale[..., None] + latter[2] * latter_scale[..., None]]
  transfers between devices with their start and end apart: 5 -> 6, of which waited for: 4 -> 3; matrix products, arithmetic and copies ran while one was open for 16% -> 0% of each run, Pallas kernels for 0% -> 12%
where the time goes in v1:
time: 120 us; the launch traced here: 118 us
  starting transfers between devices  37.2 us (31%)
  blocking collectives  27.5 us (23%)
  waiting for transfers between devices  26.8 us (22%)
  Pallas kernels  21.7 us (18%)
  local copies, waits for them, and re-layouts  3.11 us (3%)
    all_to_all x1, blocking collectives, per_device(): sums = lax.all_to_all(chunks, 'y', 0, 0, tiled=True)  27.5 us
    all_to_all x1, waiting for transfers between devices, per_device(): received = lax.all_to_all(share, 'seq', 0, 0, tiled=True)  11.8 us
    all_to_all x1, waiting for transfers between devices, per_device(): cached = lax.all_to_all(cached, ('y', 'core'), 0, 0, tiled=True)  11.4 us
    all_to_all x1, starting transfers between devices, per_device(): group_queries = lax.all_to_all(own, 'group', 0, 0, tiled=True)  9.25 us
    pallas_call x2, Pallas kernels, projected(): pl.pallas_call(functools.partial(project, mine), grid=(KVH // width,), in...  8.82 us
    ppermute x1, starting transfers between devices, per_device(): theirs = lax.ppermute(projected(False), 'core', swap)  8.77 us
    all_to_all x1, starting transfers between devices, per_device(): returned = lax.all_to_all(rows_passage, 'group', 0, 0, tiled=True)  5.38 us
    all_to_all x1, starting transfers between devices, per_device(): cached = lax.all_to_all(cached, ('y', 'core'), 0, 0, tiled=True)  4.88 us
  transfers between devices with their start and end apart: 6, of which 3 were waited for; matrix products, arithmetic and copies ran while one was open for 0% of the time, Pallas kernels for 12%

profile of v1, /device:TPU:1, one launch (start us, length us, event | category | flops | bytes accessed | tf_op | source)
XLA Modules:
  0.0 117.8 jit_solution(1894538825214840751)
XLA Ops:
  0.6 0.7 pad_add_fusion.where_ref
  1.3 4.4 %projection.4 = bf16[8,208,256]{2,1,0:T(8,128)(2,1)} custom-call(s32[4]{0:T(128)} %pad_add_fusion.where_ref, bf16[384,512]{1,0:T(8,128)(2,1)} %bitcast.11, bf16[512,1024]{1,0:T(8,128)(2,1)} %key_ref.4, bf16[512,1024]{1,0:T(8,128)(2,1)} %value_ref.4), custom_call_target="tpu_custom_call" | custom-call | flops 402653184 | bytes 4194304 | tf_op jit(solution)/shard_map/projection/pallas_call | solution.py:321
  5.7 8.8 %collective-permute-start = (bf16[8,208,256]{2,1,0:T(8,128)(2,1)}, bf16[8,208,256]{2,1,0:T(8,128)(2,1)S(1)}, u32[]{:S(2)}, u32[]{:S(2)}) collective-permute-start(bf16[8,208,256]{2,1,0:T(8,128)(2,1)} %projection.4), channel_id=1, source_target_pairs={{0,1},{1,0},{2,3},{3,2},{4,5},{5,4},{6,7},{7,6},{8,9},{9,8},{10,11... | collective-permute-start | bytes 2555912 | tf_op jit(solution)/shard_map/projection/ppermute | solution.py:337
  14.5 4.4 %projection.3.mine_ref = bf16[8,208,256]{2,1,0:T(8,128)(2,1)} custom-call(s32[4]{0:T(128)} %pad_add_fusion.where_ref, bf16[384,512]{1,0:T(8,128)(2,1)} %bitcast.12, bf16[512,1024]{1,0:T(8,128)(2,1)} %key_ref.4, bf16[512,1024]{1,0:T(8,128)(2,1)} %value_ref.4), custom_call_target="tpu_custom_call" | custom-call | flops 402653184 | bytes 4194304 | tf_op jit(solution)/shard_map/projection/pallas_call | solution.py:321
  18.9 0.0 collective-permute-done.other_ref
  18.9 1.2 copy-done
  20.1 0.2 projection.5
  20.3 0.0 copy-start.3
  20.3 0.0 copy-start.4
  20.3 0.0 copy-start.5
  20.3 27.5 %all_to_all.25.sums_ref = bf16[8,208,256]{2,1,0:T(8,128)(2,1)S(1)} all-to-all(bf16[8,208,256]{2,1,0:T(8,128)(2,1)S(1)} %projection.5), channel_id=1, replica_groups=mesh['group'=4,'seq'=8,'y'=8,'core'=2] {'y'}, dimensions={0} | all-to-all | bytes 1703936 | tf_op jit(solution)/shard_map/projection/all_to_all | solution.py:346
  47.8 0.0 copy-done.3
  47.9 1.8 %share.1 = bf16[8,192,256]{2,1,0:T(8,128)(2,1)} custom-call(s32[4]{0:T(128)S(1)} %copy-done.4, bf16[8,208,256]{2,1,0:T(8,128)(2,1)S(1)} %all_to_all.25.sums_ref, f32[2,384,128]{2,1,0:T(8,128)S(1)} %copy-done.3, f32[2,8,128]{2,1,0:T(8,128)S(1)} %copy-done.5), custom_call_target="tpu_custom_call" | custom-call | flops 1048576 | bytes 1048576 | tf_op jit(solution)/shard_map/share/pallas_call | solution.py:349
  49.7 4.8 %all-to-all-start.1 = ((bf16[8,192,256]{2,1,0:T(8,128)(2,1)}), bf16[8,192,256]{2,1,0:T(8,128)(2,1)S(1)}, u32[]{:S(2)}, u32[]{:S(2)}) async-start(bf16[8,192,256]{2,1,0:T(8,128)(2,1)} %share.1), calls=%async_computation.1 | async-start | bytes 1572864 | tf_op jit(solution)/shard_map/share/all_to_all | solution.py:357
  54.4 0.0 copy-start.1
  54.5 11.8 %all-to-all-done.1 = bf16[8,192,256]{2,1,0:T(8,128)(2,1)S(1)} async-done(((bf16[8,192,256]{2,1,0:T(8,128)(2,1)}), bf16[8,192,256]{2,1,0:T(8,128)(2,1)S(1)}, u32[]{:S(2)}, u32[]{:S(2)}) %all-to-all-start.1) | async-done | bytes 786464 | tf_op jit(solution)/shard_map/share/all_to_all | solution.py:357
  66.4 0.6 broadcast_in_dim.10
  67.0 9.3 %all-to-all-start.2 = ((f32[4,8,512]{2,1,0:T(8,128)}), f32[4,8,512]{2,1,0:T(8,128)S(1)}, u32[]{:S(2)}, u32[]{:S(2)}) async-start(f32[4,8,512]{2,1,0:T(8,128)} %broadcast_in_dim.10), calls=%async_computation.2 | async-start | bytes 131072 | tf_op jit(solution)/shard_map/decode_query_exchange/all_to_all | solution.py:314
  76.3 4.1 %collective-permute-start.1 = (bf16[1536,256]{1,0:T(8,128)(2,1)S(1)}, bf16[1536,256]{1,0:T(8,128)(2,1)S(1)}, u32[]{:S(2)}, u32[]{:S(2)}) collective-permute-start(bf16[1536,256]{1,0:T(8,128)(2,1)S(1)} %bitcast.7), channel_id=1, source_target_pairs={{0,1},{1,0},{2,3},{3,2},{4,5},{5,4},{6,7},{7,6},{8,9},{9,8},{10,11... | collective-permute-start | bytes 2359304 | tf_op jit(solution)/shard_map/passage_rows/ppermute | solution.py:375
  80.4 0.0 copy-start.6
  80.5 0.6 copy-done.6
  81.1 4.0 %cache.1 = f32[16,40,128]{2,1,0:T(8,128)} custom-call(s32[4]{0:T(128)S(1)} %copy-done.4, s32[2]{0:T(128)S(1)} %copy-done.6, f32[8,8192]{1,0:T(8,128)S(1)} %reshape.19.query_ref, f32[8,2048]{1,0:T(8,128)S(1)} %reshape.20.new_ref, bf16[2,128,1024]{2,1,0:T(8,128)(2,1)S(1)} %copy-done.1, bf16[2,128,1024]{2,1,0:T(8,128)(2,1)S(1)} %copy-done.2), custom_call_target="tpu_custom_call" | custom-call | flops 67108864 | bytes 2097152 | tf_op jit(solution)/shard_map/cache/pallas_call | solution.py:362
  85.1 0.0 all-to-all-done.2.query_ref
  85.1 4.9 %all-to-all-start.4 = ((f32[16,40,128]{2,1,0:T(8,128)}), f32[16,40,128]{2,1,0:T(8,128)S(1)}, u32[]{:S(2)}, u32[]{:S(2)}) async-start(f32[16,40,128]{2,1,0:T(8,128)} %cache.1), calls=%async_computation.4 | async-start | bytes 655360 | tf_op jit(solution)/shard_map/cache/all_to_all | solution.py:371
  90.0 0.0 collective-permute-done.1.other_ref
  90.0 1.6 %passage_rows.1 = f32[4,40,128]{2,1,0:T(8,128)} custom-call(f32[4,8,512]{2,1,0:T(8,128)S(1)} %all-to-all-done.2.query_ref, bf16[1536,256]{1,0:T(8,128)(2,1)S(1)} %bitcast.8, bf16[1536,256]{1,0:T(8,128)(2,1)S(1)} %collective-permute-done.1.other_ref), custom_call_target="tpu_custom_call" | custom-call | flops 201326592 | bytes 2097152 | tf_op jit(solution)/shard_map/passage_rows/pallas_call | solution.py:376
  91.6 11.4 %all-to-all-done.4.caches_ref = f32[16,40,128]{2,1,0:T(8,128)S(1)} async-done(((f32[16,40,128]{2,1,0:T(8,128)}), f32[16,40,128]{2,1,0:T(8,128)S(1)}, u32[]{:S(2)}, u32[]{:S(2)}) %all-to-all-start.4) | async-done | bytes 327712 | tf_op jit(solution)/shard_map/cache/all_to_all | solution.py:371
  103.0 5.4 %all-to-all-start.3 = ((f32[4,40,128]{2,1,0:T(8,128)}), f32[4,40,128]{2,1,0:T(8,128)S(1)}, u32[]{:S(2)}, u32[]{:S(2)}) async-start(f32[4,40,128]{2,1,0:T(8,128)} %passage_rows.1), calls=%async_computation.3 | async-start | bytes 163840 | tf_op jit(solution)/shard_map/passage_rows/all_to_all | solution.py:384
  108.4 4.0 %passage_attention.1 = bf16[384,512]{1,0:T(8,128)(2,1)} custom-call(s32[4]{0:T(128)S(1)} %copy-done.4, bf16[384,512]{1,0:T(8,128)(2,1)S(1)} %bitcast.10, f32[2,384,128]{2,1,0:T(8,128)S(1)} %copy-done.3, f32[2,8,128]{2,1,0:T(8,128)S(1)} %copy-done.5, bf16[1536,256]{1,0:T(8,128)(2,1)S(1)} %bitcast.9, bf16[1536,256]{1,0:T(8,128)(2,1)S(1)} %collective-permute-done.1.other_ref), custom_call_target="tpu_custom_call" | custom-call | flops 9663676416 | bytes 3145728 | tf_op jit(solution)/shard_map/passage_attention/pallas_call | solution.py:387
  112.4 3.5 %all-to-all-done.3.passages_ref = f32[4,40,128]{2,1,0:T(8,128)S(1)} async-done(((f32[4,40,128]{2,1,0:T(8,128)}), f32[4,40,128]{2,1,0:T(8,128)S(1)}, u32[]{:S(2)}, u32[]{:S(2)}) %all-to-all-start.3) | async-done | bytes 81952 | tf_op jit(solution)/shard_map/passage_rows/all_to_all | solution.py:384
  115.9 1.3 %row_merge.1 = f32[8,512]{1,0:T(8,128)S(1)} custom-call(s32[2]{0:T(128)S(1)} %copy-done.7, f32[4,40,128]{2,1,0:T(8,128)S(1)} %all-to-all-done.3.passages_ref, f32[16,40,128]{2,1,0:T(8,128)S(1)} %all-to-all-done.4.caches_ref), custom_call_target="tpu_custom_call" | custom-call | flops 1048576 | bytes 1048576 | tf_op jit(solution)/shard_map/row_merge/pallas_call | solution.py:402
  117.2 0.6 reshape.18
  (21 shorter events, 0.2 us)
Async XLA Ops:
  5.7 13.2 %collective-permute-start = (bf16[8,208,256]{2,1,0:T(8,128)(2,1)}, bf16[8,208,256]{2,1,0:T(8,128)(2,1)S(1)}, u32[]{:S(2)}, u32[]{:S(2)}) collective-permute-start(bf16[8,208,256]{2,1,0:T(8,128)(2,1)} %projection.4), channel_id=1, source_target_pairs={{0,1},{1,0},{2,3},{3,2},{4,5},{5,4},{6,7},{7,6},{8,9},{9,8},{10,11... | collective-permute-start | bytes 2555912 | tf_op jit(solution)/shard_map/projection/ppermute | solution.py:337
  18.9 1.2 copy-start
  20.3 27.6 %copy-start.3 = (f32[2,384,128]{2,1,0:T(8,128)S(1)}, f32[2,384,128]{2,1,0:T(8,128)}, u32[]{:S(2)}) copy-start(f32[2,384,128]{2,1,0:T(8,128)} %constant.26.clone.near_ref) | copy-start | bytes 1179652
  20.3 27.6 %copy-start.4 = (s32[4]{0:T(128)S(1)}, s32[4]{0:T(128)}, u32[]{:S(2)}) copy-start(s32[4]{0:T(128)} %pad_add_fusion.where_ref) | copy-start | bytes 52
  20.3 27.6 %copy-start.5 = (f32[2,8,128]{2,1,0:T(8,128)S(1)}, f32[2,8,128]{2,1,0:T(8,128)}, u32[]{:S(2)}) copy-start(f32[2,8,128]{2,1,0:T(8,128)} %constant.27.clone.far_ref) | copy-start | bytes 24580
  49.6 4.8 %copy-start.9 = (bf16[4,2,8192]{2,1,0:T(2,128)(2,1)S(1)}, bf16[4,2,8192]{2,1,0:T(2,128)(2,1)}, u32[]{:S(2)}) copy-start(bf16[4,2,8192]{2,1,0:T(2,128)(2,1)} %param.17) | copy-start | bytes 393220
  49.6 30.8 %copy-start.2 = (bf16[2,128,1024]{2,1,0:T(8,128)(2,1)S(1)}, bf16[2,128,1024]{2,1,0:T(8,128)(2,1)}, u32[]{:S(2)}) copy-start(bf16[2,128,1024]{2,1,0:T(8,128)(2,1)} %value_ref.5) | copy-start | bytes 1572868
  49.7 16.7 %all-to-all-start.1 = ((bf16[8,192,256]{2,1,0:T(8,128)(2,1)}), bf16[8,192,256]{2,1,0:T(8,128)(2,1)S(1)}, u32[]{:S(2)}, u32[]{:S(2)}) async-start(bf16[8,192,256]{2,1,0:T(8,128)(2,1)} %share.1), calls=%async_computation.1 | async-start | bytes 1572864 | tf_op jit(solution)/shard_map/share/all_to_all | solution.py:357
  54.4 26.0 %copy-start.1 = (bf16[2,128,1024]{2,1,0:T(8,128)(2,1)S(1)}, bf16[2,128,1024]{2,1,0:T(8,128)(2,1)}, u32[]{:S(2)}) copy-start(bf16[2,128,1024]{2,1,0:T(8,128)(2,1)} %key_ref.5) | copy-start | bytes 1572868
  67.0 13.4 %copy-start.10 = (bf16[4,2,1024]{2,1,0:T(2,128)(2,1)S(1)}, bf16[4,2,1024]{2,1,0:T(2,128)(2,1)}, u32[]{:S(2)}) copy-start(bf16[4,2,1024]{2,1,0:T(2,128)(2,1)} %param.19) | copy-start | bytes 49156
  67.0 13.4 %copy-start.11 = (bf16[4,2,1024]{2,1,0:T(2,128)(2,1)S(1)}, bf16[4,2,1024]{2,1,0:T(2,128)(2,1)}, u32[]{:S(2)}) copy-start(bf16[4,2,1024]{2,1,0:T(2,128)(2,1)} %param.18) | copy-start | bytes 49156
  67.0 18.1 %all-to-all-start.2 = ((f32[4,8,512]{2,1,0:T(8,128)}), f32[4,8,512]{2,1,0:T(8,128)S(1)}, u32[]{:S(2)}, u32[]{:S(2)}) async-start(f32[4,8,512]{2,1,0:T(8,128)} %broadcast_in_dim.10), calls=%async_computation.2 | async-start | bytes 131072 | tf_op jit(solution)/shard_map/decode_query_exchange/all_to_all | solution.py:314
  76.3 13.8 %collective-permute-start.1 = (bf16[1536,256]{1,0:T(8,128)(2,1)S(1)}, bf16[1536,256]{1,0:T(8,128)(2,1)S(1)}, u32[]{:S(2)}, u32[]{:S(2)}) collective-permute-start(bf16[1536,256]{1,0:T(8,128)(2,1)S(1)} %bitcast.7), channel_id=1, source_target_pairs={{0,1},{1,0},{2,3},{3,2},{4,5},{5,4},{6,7},{7,6},{8,9},{9,8},{10,11... | collective-permute-start | bytes 2359304 | tf_op jit(solution)/shard_map/passage_rows/ppermute | solution.py:375
  80.4 0.7 copy-start.6
  85.1 17.9 %all-to-all-start.4 = ((f32[16,40,128]{2,1,0:T(8,128)}), f32[16,40,128]{2,1,0:T(8,128)S(1)}, u32[]{:S(2)}, u32[]{:S(2)}) async-start(f32[16,40,128]{2,1,0:T(8,128)} %cache.1), calls=%async_computation.4 | async-start | bytes 655360 | tf_op jit(solution)/shard_map/cache/all_to_all | solution.py:371
  90.0 18.4 %copy-start.8 = (bf16[1,384,512]{2,1,0:T(8,128)(2,1)S(1)}, bf16[1,384,512]{2,1,0:T(8,128)(2,1)}, u32[]{:S(2)}) copy-start(bf16[1,384,512]{2,1,0:T(8,128)(2,1)} %param.14) | copy-start | bytes 1179652
  103.0 12.9 %all-to-all-start.3 = ((f32[4,40,128]{2,1,0:T(8,128)}), f32[4,40,128]{2,1,0:T(8,128)S(1)}, u32[]{:S(2)}, u32[]{:S(2)}) async-start(f32[4,40,128]{2,1,0:T(8,128)} %passage_rows.1), calls=%async_computation.3 | async-start | bytes 163840 | tf_op jit(solution)/shard_map/passage_rows/all_to_all | solution.py:384
  108.4 7.5 %copy-start.7 = (s32[2]{0:T(128)S(1)}, s32[2]{0:T(128)}, u32[]{:S(2)}) copy-start(s32[2]{0:T(128)} %passage_ref.1) | copy-start | bytes 28

commit v2 on v1

--- a/solution.py
+++ b/solution.py
@@ -17,7 +17,6 @@
 HALF = 192
 HEADS = 4
 EXTRA = 16
-STATE = 40
 ROPE_BASE = 500000.0
 NORM_EPS = 1e-05
 NEG = -1e30
@@ -54,36 +53,51 @@
     return x * cosine + pltpu.roll(x, HS // 2, 1) * sine
 
 
-def project(mine, where_ref, hidden_ref, key_ref, value_ref, out_ref, squares_ref):
-    core = where_ref[1] if mine else 1 - where_ref[1]
-    rows = pl.ds(pl.multiple_of(core * HALF, HALF), HALF)
+def project(where_ref, hidden_ref, key_ref, value_ref, mine_ref, theirs_ref, squares_ref):
+    core = where_ref[1]
 
     @pl.when(pl.program_id(0) == 0)
     def _():
-        h = hidden_ref[rows, :].astype(f32)
+        h = hidden_ref[...].astype(f32)
         sq = h * h
         high = sq.astype(bf16)
         low = (sq - high.astype(f32)).astype(bf16)
         ones = jnp.ones((EXTRA, hidden_ref.shape[1]), bf16)
-        sums = dot_t(ones, high) + dot_t(ones, low)
-        sums = jnp.concatenate([sums, jnp.zeros((EXTRA, 256 - HALF), f32)], axis=1)
         row = lax.broadcasted_iota(jnp.int32, (EXTRA, 256), 0)
-        squares_ref[...] = jnp.where(row == where_ref[2], sums, 0.0).astype(bf16)
-
-    h = hidden_ref[rows, :]
+        for half in range(2):
+            part = slice(half * HALF, (half + 1) * HALF)
+            sums = dot_t(ones, high[part]) + dot_t(ones, low[part])
+            sums = jnp.concatenate([sums, jnp.zeros((EXTRA, 256 - HALF), f32)], axis=1)
+            squares_ref[half] = jnp.where(row == where_ref[2], sums, 0.0).astype(bf16)
+
+    h = hidden_ref[...]
     keys = dot(h, key_ref[...]).astype(bf16)
     values = dot(h, value_ref[...]).astype(bf16)
-    for j in range(out_ref.shape[0]):
-        out_ref[j, :HALF, :HS] = keys[:, j * HS : (j + 1) * HS]
-        out_ref[j, :HALF, HS:] = values[:, j * HS : (j + 1) * HS]
-        out_ref[j, HALF:, :] = squares_ref[...]
+
+    def put(out_ref, half):
+        part = slice(half * HALF, (half + 1) * HALF)
+        for j in range(out_ref.shape[0]):
+            out_ref[j, :HALF, :HS] = keys[part, j * HS : (j + 1) * HS]
+            out_ref[j, :HALF, HS:] = values[part, j * HS : (j + 1) * HS]
+            out_ref[j, HALF:, :] = squares_ref[half]
+
+    @pl.when(core == 0)
+    def _():
+        put(mine_ref, 0)
+        put(theirs_ref, 1)
+
+    @pl.when(core == 1)
+    def _():
+        put(mine_ref, 1)
+        put(theirs_ref, 0)
 
 
 def add(mine_ref, other_ref, out_ref):
     out_ref[...] = (mine_ref[...].astype(f32) + other_ref[...].astype(f32)).astype(bf16)
 
 
-def finish_share(where_ref, sums_ref, near_ref, far_ref, out_ref):
+def finish_share(where_ref, sums_ref, near_ref, far_ref, before_a, before_b, out_ref):
+    del before_a, before_b
     s, core = where_ref[0], where_ref[1]
     squares, sums = 0.0, 0.0
     for k in range(sums_ref.shape[0]):
@@ -102,22 +116,41 @@
         out_ref[to] = share
 
 
-def put_state(out_ref, at, weighted, highest, totals):
-    rows = weighted.shape[0]
-    lane = lax.broadcasted_iota(jnp.int32, (rows, HS), 1)
-    both = jnp.where(lane == 0, highest, jnp.where(lane == 1, totals, 0.0))
-    flat = jnp.transpose(both)[:8, :]
-    for j in range(rows // 32):
-        out_ref[at + j, :32, :] = weighted[j * 32 : (j + 1) * 32, :]
-        out_ref[at + j, 32:, :] = jnp.concatenate(
-            [flat[:, j * 32 : (j + 1) * 32], jnp.zeros((8, HS - 32), f32)], axis=1
-        )
+def state_of(weighted, highest, totals):
+    lane = lax.broadcasted_iota(jnp.int32, weighted.shape, weighted.ndim - 1)
+    tail = jnp.where(lane < HS // 2, highest, totals)
+    return jnp.concatenate([weighted, tail], axis=-1)
+
+
+def parts_of(state):
+    return state[..., :HS], state[..., HS : HS + 1], state[..., HS + HS // 2 : HS + HS // 2 + 1]
+
+
+def merged(a, b):
+    (a_sum, a_high, a_total), (b_sum, b_high, b_total) = parts_of(a), parts_of(b)
+    highest = jnp.maximum(a_high, b_high)
+    a_factor, b_factor = jnp.exp2(a_high - highest), jnp.exp2(b_high - highest)
+    return state_of(
+        a_sum * a_factor + b_sum * b_factor, highest, a_total * a_factor + b_total * b_factor
+    )
+
+
+def merge_halves(bit, where_ref, keep_ref, other_ref, out_ref, *send_ref):
+    half = keep_ref.shape[0] // 2
+    mine = (where_ref[3] >> bit) & 1
+    keep, send = pl.ds(mine * half, half), pl.ds((1 - mine) * half, half)
+    out_ref[...] = merged(keep_ref[keep], other_ref[keep])
+    send_ref[0][...] = merged(keep_ref[send], other_ref[send])
+
+
+def merge_last(keep_ref, other_ref, out_ref):
+    out_ref[...] = merged(keep_ref[...], other_ref[...])
 
 
 def cache_states(
-    where_ref, length_ref, query_ref, new_ref, key_ref, value_ref, out_ref
+    where_ref, length_ref, query_ref, new_ref, key_ref, value_ref, keep_ref, send_ref
 ):
-    tp = where_ref[2]
+    core, tp = where_ref[1], where_ref[2]
     slots = key_ref.shape[1]
     rows = 64
     q = lax.broadcasted_iota(jnp.int32, (rows, 2 * slots), 0)
@@ -150,17 +183,18 @@
             new_weights, axis=1, keepdims=True
         )
         weighted = dot(weights.astype(bf16), values) + dot(new_weights.astype(bf16), new_values)
-        put_state(out_ref, 2 * head, weighted, highest, totals)
-
-
-def passage_states(query_ref, own_ref, other_ref, out_ref):
+        state = state_of(weighted, highest, totals)
+        keep_ref[head] = jnp.where(core == 0, state[:32], state[32:])
+        send_ref[head] = jnp.where(core == 0, state[32:], state[:32])
+
+
+def passage_states(
+    where_ref, query_ref, query1_ref, query2_ref, own_ref, other_ref, before, out_ref
+):
+    del before
+    queries = [query_ref[...], query1_ref[...], query2_ref[:8, :], query2_ref[8:, :]]
     query = jnp.concatenate(
-        [
-            query_ref[g, :, p * HS : (p + 1) * HS]
-            for g in range(query_ref.shape[0])
-            for p in range(HEADS)
-        ],
-        axis=0,
+        [rows[:, p * HS : (p + 1) * HS] for rows in queries for p in range(HEADS)], axis=0
     ).astype(bf16)
     refs = (own_ref, other_ref)
     scores = [dot_t(query, ref[:, :HS]) * SCALE2 for ref in refs]
@@ -168,7 +202,9 @@
     weights = [jnp.exp2(score - highest) for score in scores]
     totals = jnp.sum(weights[0] + weights[1], axis=1, keepdims=True)
     weighted = sum(dot(w.astype(bf16), ref[:, HS:]) for w, ref in zip(weights, refs, strict=True))
-    put_state(out_ref, 0, weighted, highest, totals)
+    state = state_of(weighted, highest, totals)
+    for r in range(4):
+        out_ref[where_ref[4] ^ r] = state[32 * r : 32 * (r + 1)]
 
 
 def attend(
@@ -239,32 +275,14 @@
         ).astype(bf16)
 
 
-def merge(passage_ref, passages_ref, caches_ref, out_ref):
-    count, sources = passages_ref.shape[0], caches_ref.shape[0]
-    tail = jnp.transpose(caches_ref[:, 32:, :].reshape(sources * 8, HS))[:32, :]
-    row = lax.broadcasted_iota(jnp.int32, (32, 1), 0) & 1
+def merge(passage_ref, passages_ref, cache_ref, out_ref):
+    row = lax.broadcasted_iota(jnp.int32, (32, 2 * HS), 0) & 1
     chosen = jnp.where(row == 1, passage_ref[1], passage_ref[0])
-    tails = jnp.concatenate(
-        [passages_ref[:, 32:, :].reshape(count * 8, HS), jnp.zeros((HS - count * 8, HS), f32)],
-        axis=0,
-    )
-    tails = jnp.transpose(tails)[:32, :]
-    highs = [tail[:, 8 * t : 8 * t + 1] for t in range(sources)]
-    totals = [tail[:, 8 * t + 1 : 8 * t + 2] for t in range(sources)]
-    states = [caches_ref[t, :32, :] for t in range(sources)]
-    high, total, state = tails[:, 0:1], tails[:, 1:2], passages_ref[0, :32, :]
-    for g in range(1, count):
-        high = jnp.where(chosen == g, tails[:, 8 * g : 8 * g + 1], high)
-        total = jnp.where(chosen == g, tails[:, 8 * g + 1 : 8 * g + 2], total)
-        state = jnp.where(chosen == g, passages_ref[g, :32, :], state)
-    highest = functools.reduce(jnp.maximum, highs, high)
-    factor = jnp.exp2(high - highest)
-    total, state = total * factor, state * factor
-    for t in range(sources):
-        factor = jnp.exp2(highs[t] - highest)
-        total = total + totals[t] * factor
-        state = state + states[t] * factor
-    context = state / total
+    state = passages_ref[0]
+    for g in range(1, passages_ref.shape[0]):
+        state = jnp.where(chosen == g, passages_ref[g], state)
+    weighted, _, total = parts_of(merged(state, cache_ref[0]))
+    context = weighted / total
     for p in range(HEADS):
         out_ref[:, p * HS : (p + 1) * HS] = context[p * 8 : (p + 1) * 8, :]
 
@@ -302,111 +320,163 @@
 ):
     near, far = tables()
     core, y, s = lax.axis_index("core"), lax.axis_index("y"), lax.axis_index("seq")
-    groups = lax.axis_size("group")
+    group, groups, ys = lax.axis_index("group"), lax.axis_size("group"), lax.axis_size("y")
     tp = y * 2 + core
-    where = jnp.stack([s, core, tp, tp]).astype(jnp.int32)
+    where = jnp.stack([s, core, tp, y, group, s, s, s]).astype(jnp.int32)
     features = hidden.shape[2]
+    swap = [(0, 1), (1, 0)]
+    state = (32, 2 * HS)
+
+    def call(kernel, out, scalars, arrays, *operands, spaces=(), mib=32, **more):
+        single = not isinstance(out, list)
+        result = pl.pallas_call(
+            kernel,
+            in_specs=smem(scalars) + vmem(arrays) + list(spaces),
+            out_specs=vmem(1 if single else len(out)),
+            out_shape=[out] if single else out,
+            compiler_params=params(mib),
+            **more,
+        )(*operands)
+        return result[0] if single else result
+
+    shape = jax.ShapeDtypeStruct
+    hbm = pl.BlockSpec(memory_space=pl.ANY)
+
+    with jax.named_scope("projection"):
+        width = 2
+        block = pl.BlockSpec((width, HALF + EXTRA, 2 * HS), lambda i: (i, 0, 0))
+        chunk = shape((KVH, HALF + EXTRA, 2 * HS), bf16)
+        mine, theirs = pl.pallas_call(
+            project,
+            grid=(KVH // width,),
+            in_specs=smem(1)
+            + [
+                pl.BlockSpec((TOK, features), lambda i: (0, 0)),
+                pl.BlockSpec((features, width * HS), lambda i: (0, i)),
+                pl.BlockSpec((features, width * HS), lambda i: (0, i)),
+            ],
+            out_specs=[block, block],
+            out_shape=[chunk, chunk],
+            scratch_shapes=[pltpu.VMEM((2, EXTRA, 256), bf16)],
+            compiler_params=params(56),
+            cost_estimate=cost(2 * TOK * features * 2048, 0, 4 << 20),
+        )(where, hidden[0], key_weight, value_weight)
+        theirs = lax.ppermute(theirs, "core", swap)
+        chunks = call(add, chunk, 0, 2, mine, theirs, cost_estimate=cost(1 << 20))
+        sums = lax.all_to_all(chunks, "y", 0, 0, tiled=True)
 
     with jax.named_scope("decode_query_exchange"):
         queries = decode_queries.reshape(8, -1).astype(f32)
         own = lax.dynamic_slice_in_dim(queries, tp * HEADS * HS, HEADS * HS, 1)
-        own = jnp.broadcast_to(own[None], (groups, 8, HEADS * HS))
-        group_queries = lax.all_to_all(own, "group", 0, 0, tiled=True)
-
-    swap = [(0, 1), (1, 0)]
-    with jax.named_scope("projection"):
-        width = 2
-
-        def projected(mine):
-            return pl.pallas_call(
-                functools.partial(project, mine),
-                grid=(KVH // width,),
-                in_specs=smem(1)
-                + [
-                    pl.BlockSpec((TOK, features), lambda i: (0, 0)),
-                    pl.BlockSpec((features, width * HS), lambda i: (0, i)),
-                    pl.BlockSpec((features, width * HS), lambda i: (0, i)),
-                ],
-                out_specs=pl.BlockSpec((width, HALF + EXTRA, 2 * HS), lambda i: (i, 0, 0)),
-                out_shape=jax.ShapeDtypeStruct((KVH, HALF + EXTRA, 2 * HS), bf16),
-                scratch_shapes=[pltpu.VMEM((EXTRA, 256), bf16)],
-                compiler_params=params(56),
-                cost_estimate=cost(TOK * features * 2048, 0, 4 << 20),
-            )(where, hidden[0], key_weight, value_weight)
-
-        theirs = lax.ppermute(projected(False), "core", swap)
-        chunks = pl.pallas_call(
-            add,
-            in_specs=vmem(2),
-            out_specs=vmem(1)[0],
-            out_shape=jax.ShapeDtypeStruct((KVH, HALF + EXTRA, 2 * HS), bf16),
-            compiler_params=params(32),
-            cost_estimate=cost(1 << 20),
-        )(projected(True), theirs)
-        sums = lax.all_to_all(chunks, "y", 0, 0, tiled=True)
-
-    with jax.named_scope("share"):
-        share = pl.pallas_call(
-            finish_share,
-            in_specs=smem(1) + vmem(3),
-            out_specs=vmem(1)[0],
-            out_shape=jax.ShapeDtypeStruct((SEQ, HALF, 2 * HS), bf16),
-            compiler_params=params(32),
-            cost_estimate=cost(1 << 20),
-        )(where, sums, near, far)
-        received = lax.all_to_all(share, "seq", 0, 0, tiled=True)
+        near_group = lax.ppermute(own, "group", [(g, g ^ 1) for g in range(groups)])
+        far_groups = lax.ppermute(
+            jnp.concatenate([own, near_group]), "group", [(g, g ^ 2) for g in range(groups)]
+        )
 
     with jax.named_scope("cache"):
         news = jnp.concatenate([new_keys, new_values], axis=2).reshape(8, -1).astype(f32)
-        news, queries, _ = lax.optimization_barrier((news, queries, chunks))
-        cached = pl.pallas_call(
+        keep, send = call(
             cache_states,
-            in_specs=smem(2) + vmem(4),
-            out_specs=vmem(1)[0],
-            out_shape=jax.ShapeDtypeStruct((16, STATE, HS), f32),
-            compiler_params=params(32),
+            [shape((KVH, *state), f32)] * 2,
+            2,
+            4,
+            where,
+            cache_lengths,
+            queries,
+            news,
+            cache_keys,
+            cache_values,
             cost_estimate=cost(8 * 64 * 256 * 128 * 4, 8 * 64 * 256, 2 << 20),
-        )(where, cache_lengths, queries, news, cache_keys, cache_values)
-        cached, _ = lax.optimization_barrier((cached, share))
-        cached = lax.all_to_all(cached, ("y", "core"), 0, 0, tiled=True)
+        )
+        other = lax.ppermute(send, "core", swap)
+        for bit in (2, 1, 0):
+            half = keep.shape[0] // 2
+            keep, send = call(
+                functools.partial(merge_halves, bit),
+                [shape((half, *state), f32)] * 2,
+                1,
+                2,
+                where,
+                keep,
+                other,
+                cost_estimate=cost(1 << 18),
+            )
+            other = lax.ppermute(send, "y", [(i, i ^ (1 << bit)) for i in range(ys)])
+            if bit == 2:
+                early = other
+        cached = call(
+            merge_last, shape((1, *state), f32), 0, 2, keep, other, cost_estimate=cost(1 << 16)
+        )
+
+    with jax.named_scope("share"):
+        share = call(
+            finish_share,
+            shape((SEQ, HALF, 2 * HS), bf16),
+            1,
+            3,
+            where,
+            sums,
+            near,
+            far,
+            far_groups,
+            early,
+            spaces=(hbm, hbm),
+            cost_estimate=cost(1 << 20),
+        )
+        received = lax.all_to_all(share, "seq", 0, 0, tiled=True)
 
     with jax.named_scope("passage_rows"):
-        own_kv = received.reshape(SEQ * HALF, 2 * HS)
+        own_kv, _ = lax.optimization_barrier((received.reshape(SEQ * HALF, 2 * HS), cached))
         other_kv = lax.ppermute(own_kv, "core", swap)
-        rows_passage = pl.pallas_call(
+        rows_passage = call(
             passage_states,
-            in_specs=vmem(3),
-            out_specs=vmem(1)[0],
-            out_shape=jax.ShapeDtypeStruct((groups, STATE, HS), f32),
-            compiler_params=params(32),
+            shape((groups, *state), f32),
+            1,
+            5,
+            where,
+            own,
+            near_group,
+            far_groups,
+            own_kv,
+            other_kv,
+            cached,
+            spaces=(hbm,),
             cost_estimate=cost(128 * 3072 * 128 * 4, 128 * 3072, 2 << 20),
-        )(group_queries, own_kv, other_kv)
+        )
         returned = lax.all_to_all(rows_passage, "group", 0, 0, tiled=True)
 
     with jax.named_scope("passage_attention"):
-        passage_out = pl.pallas_call(
+        passage_out = call(
             attend,
-            in_specs=smem(1) + vmem(5),
-            out_specs=vmem(1)[0],
-            out_shape=jax.ShapeDtypeStruct((TOK, HEADS * HS), bf16),
+            shape((TOK, HEADS * HS), bf16),
+            1,
+            5,
+            where,
+            passage_queries[0],
+            near,
+            far,
+            own_kv,
+            other_kv,
+            mib=48,
             scratch_shapes=[
                 pltpu.VMEM((HEADS, TOK, HS), f32),
                 pltpu.VMEM((HEADS, TOK, 2 * HS), f32),
                 pltpu.VMEM((HEADS, TOK, HS), bf16),
             ],
-            compiler_params=params(48),
             cost_estimate=cost(1536 * 3072 * 128 * 4 * 4, 1536 * 3072, 3 << 20),
-        )(where, passage_queries[0], near, far, own_kv, other_kv)
+        )
 
     with jax.named_scope("row_merge"):
-        row_out = pl.pallas_call(
+        row_out = call(
             merge,
-            in_specs=smem(1) + vmem(2),
-            out_specs=vmem(1)[0],
-            out_shape=jax.ShapeDtypeStruct((8, HEADS * HS), f32),
-            compiler_params=params(32),
+            shape((8, HEADS * HS), f32),
+            1,
+            2,
+            passage_of_row,
+            returned,
+            cached,
             cost_estimate=cost(1 << 20),
-        )(passage_of_row, returned, cached)
+        )
     return passage_out[None], row_out.astype(bf16).reshape(4, 2, HEADS * HS)
 
 

time: 120 us -> 104 us (0.87)
  the two profiles are of different devices: /device:TPU:1 before, /device:TPU:7 now
where the time goes in v2:
time: 104 us; the launch traced here: 103 us
  starting transfers between devices  58.2 us (56%)
  Pallas kernels  27.7 us (27%)
  waiting for transfers between devices  13 us (12%)
  local copies, waits for them, and re-layouts  3.42 us (3%)
    pallas_call x10, Pallas kernels, call(): pl.pallas_call(kernel, in_specs=smem(scalars) + vmem(arrays) + list(space...  22.7 us
    ppermute x3, starting transfers between devices, per_device(): other = lax.ppermute(send, 'y', [(i, i ^ 1 << bit) for i in range(ys)])  11.5 us
    ppermute x1, starting transfers between devices, per_device(): lax.ppermute(jnp.concatenate([own, near_group]), 'group', [(g, g ^ 2) for...  8.84 us
    all_to_all x1, starting transfers between devices, per_device(): returned = lax.all_to_all(rows_passage, 'group', 0, 0, tiled=True)  8.35 us
    ppermute x3, waiting for transfers between devices, per_device(): other = lax.ppermute(send, 'y', [(i, i ^ 1 << bit) for i in range(ys)])  7.62 us
    all_to_all x1, starting transfers between devices, per_device(): sums = lax.all_to_all(chunks, 'y', 0, 0, tiled=True)  6.96 us
    ppermute x1, starting transfers between devices, per_device(): near_group = lax.ppermute(own, 'group', [(g, g ^ 1) for g in range(groups)])  5.81 us
    ppermute x1, starting transfers between devices, per_device(): other_kv = lax.ppermute(own_kv, 'core', swap)  5.76 us
  transfers between devices with their start and end apart: 11, of which 5 were waited for; matrix products, arithmetic and copies ran while one was open for 0% of the time, Pallas kernels for 16%

profile of v2, /device:TPU:7, one launch (start us, length us, event | category | flops | bytes accessed | tf_op | source)
XLA Modules:
  0.0 103.3 jit_solution(18091951693351863450)
XLA Ops:
  0.6 0.7 stack.26.where_ref
  1.3 5.0 %projection.2 = (bf16[8,208,256]{2,1,0:T(8,128)(2,1)}, bf16[8,208,256]{2,1,0:T(8,128)(2,1)}) custom-call(s32[8]{0:T(128)} %stack.26.where_ref, bf16[384,512]{1,0:T(8,128)(2,1)} %bitcast.13, bf16[512,1024]{1,0:T(8,128)(2,1)} %key_ref.2, bf16[512,1024]{1,0:T(8,128)(2,1)} %value_ref.2), custom_call_target="tpu_custom_call" | custom-call | flops 805306368 | bytes 4194304 | tf_op jit(solution)/shard_map/projection/pallas_call | solution.py:349
  6.3 2.6 %collective-permute-start = (bf16[8,208,256]{2,1,0:T(8,128)(2,1)}, bf16[8,208,256]{2,1,0:T(8,128)(2,1)S(1)}, u32[]{:S(2)}, u32[]{:S(2)}) collective-permute-start(bf16[8,208,256]{2,1,0:T(8,128)(2,1)} %get-tuple-element.14), channel_id=1, source_target_pairs={{0,1},{1,0},{2,3},{3,2},{4,5},{5,4},{6,7},{7,6},{8,9},{9,8},{10,11... | collective-permute-start | bytes 2555912 | tf_op jit(solution)/shard_map/projection/ppermute | solution.py:364
  8.9 2.2 %collective-permute-done.other_ref = bf16[8,208,256]{2,1,0:T(8,128)(2,1)S(1)} collective-permute-done((bf16[8,208,256]{2,1,0:T(8,128)(2,1)}, bf16[8,208,256]{2,1,0:T(8,128)(2,1)S(1)}, u32[]{:S(2)}, u32[]{:S(2)}) %collective-permute-start) | collective-permute-done | bytes 852000 | tf_op jit(solution)/shard_map/projection/ppermute | solution.py:364
  11.1 1.2 %copy-done = bf16[8,208,256]{2,1,0:T(8,128)(2,1)S(1)} copy-done((bf16[8,208,256]{2,1,0:T(8,128)(2,1)S(1)}, bf16[8,208,256]{2,1,0:T(8,128)(2,1)}, u32[]{:S(2)}) %copy-start) | copy-done | bytes 851992
  12.3 1.1 %projection.3 = bf16[8,208,256]{2,1,0:T(8,128)(2,1)} custom-call(bf16[8,208,256]{2,1,0:T(8,128)(2,1)S(1)} %copy-done, bf16[8,208,256]{2,1,0:T(8,128)(2,1)S(1)} %collective-permute-done.other_ref), custom_call_target="tpu_custom_call" | custom-call | flops 1048576 | bytes 1048576 | tf_op jit(solution)/shard_map/projection/pallas_call | solution.py:332
  13.4 7.0 %all-to-all-start = ((bf16[8,208,256]{2,1,0:T(8,128)(2,1)}), bf16[8,208,256]{2,1,0:T(8,128)(2,1)S(1)}, u32[]{:S(2)}, u32[]{:S(2)}) async-start(bf16[8,208,256]{2,1,0:T(8,128)(2,1)} %projection.3), calls=%async_computation | async-start | bytes 1703936 | tf_op jit(solution)/shard_map/projection/all_to_all | solution.py:366
  20.6 0.8 copy-done.1
  21.4 2.7 %cache.5 = (f32[8,32,256]{2,1,0:T(8,128)S(1)}, f32[8,32,256]{2,1,0:T(8,128)S(1)}) custom-call(s32[8]{0:T(128)S(1)} %copy-done.4, s32[2]{0:T(128)S(1)} %copy-done.6, f32[8,8192]{1,0:T(8,128)S(1)} %reshape.18.query_ref, f32[8,2048]{1,0:T(8,128)S(1)} %reshape.19.new_ref, bf16[2,128,1024]{2,1,0:T(8,128)(2,1)S(1)} %copy-done.1, bf16[2,128,1024]{2,1,0:T(8,128)(2,1)S(1)} %copy-done.2), custom_call_target="tpu_custom_call" | custom-call | flops 67108864 | bytes 2097152 | tf_op jit(solution)/shard_map/cache/pallas_call | solution.py:332
  24.1 2.7 %collective-permute-start.3 = (f32[8,32,256]{2,1,0:T(8,128)S(1)}, f32[8,32,256]{2,1,0:T(8,128)S(1)}, u32[]{:S(2)}, u32[]{:S(2)}) collective-permute-start(f32[8,32,256]{2,1,0:T(8,128)S(1)} %get-tuple-element.16), channel_id=1, source_target_pairs={{0,1},{1,0},{2,3},{3,2},{4,5},{5,4},{6,7},{7,6},{8,9},{9,8},{10,11... | collective-permute-start | bytes 786440 | tf_op jit(solution)/shard_map/cache/ppermute | solution.py:391
  26.9 5.8 %collective-permute-start.1 = (f32[8,512]{1,0:T(8,128)S(1)}, f32[8,512]{1,0:T(8,128)S(1)}, u32[]{:S(2)}, u32[]{:S(2)}) collective-permute-start(f32[8,512]{1,0:T(8,128)S(1)} %constant_dynamic-slice_fusion.query_ref), channel_id=1, source_target_pairs={{0,128},{128,0},{256,384},{384,256},{1,129},{129,1},{257,385},{385... | collective-permute-start | bytes 49160 | tf_op jit(solution)/shard_map/decode_query_exchange/ppermute | solution.py:371
  32.7 0.9 cache.6
  33.6 0.0 copy-start.5
  33.6 7.6 %collective-permute-start.4 = (f32[4,32,256]{2,1,0:T(8,128)S(1)}, f32[4,32,256]{2,1,0:T(8,128)S(1)}, u32[]{:S(2)}, u32[]{:S(2)}) collective-permute-start(f32[4,32,256]{2,1,0:T(8,128)S(1)} %get-tuple-element.17), channel_id=1, source_target_pairs={{0,8},{2,10},{4,12},{6,14},{8,0},{10,2},{12,4},{14,6},{1,9},{3,11}... | collective-permute-start | bytes 393224 | tf_op jit(solution)/shard_map/cache/ppermute | solution.py:404
  41.2 8.8 %collective-permute-start.2 = (f32[16,512]{1,0:T(8,128)S(1)}, f32[16,512]{1,0:T(8,128)S(1)}, u32[]{:S(2)}, u32[]{:S(2)}) collective-permute-start(f32[16,512]{1,0:T(8,128)S(1)} %pad_maximum_fusion), channel_id=1, source_target_pairs={{0,256},{128,384},{256,0},{384,128},{1,257},{129,385},{257,1},{385... | collective-permute-start | bytes 98312 | tf_op jit(solution)/shard_map/decode_query_exchange/ppermute | solution.py:372
  50.0 1.3 %collective-permute-done.2.before_a.query2_ref = f32[16,512]{1,0:T(8,128)S(1)} collective-permute-done((f32[16,512]{1,0:T(8,128)S(1)}, f32[16,512]{1,0:T(8,128)S(1)}, u32[]{:S(2)}, u32[]{:S(2)}) %collective-permute-start.2) | collective-permute-done | bytes 32800 | tf_op jit(solution)/shard_map/decode_query_exchange/ppermute | solution.py:372
  51.3 1.8 %share.1 = bf16[8,192,256]{2,1,0:T(8,128)(2,1)} custom-call(s32[8]{0:T(128)S(1)} %copy-done.4, bf16[8,208,256]{2,1,0:T(8,128)(2,1)S(1)} %all-to-all-done.sums_ref, f32[2,384,128]{2,1,0:T(8,128)S(1)} %copy-done.3, f32[2,8,128]{2,1,0:T(8,128)S(1)} %copy-done.5, f32[16,512]{1,0:T(8,128)S(1)} %collective-permute-done.2.before_a.query2_ref, ...), custom_call_target="tpu_custom_call" | custom-call | flops 1048576 | bytes 1048576 | tf_op jit(solution)/shard_map/share/pallas_call | solution.py:332
  53.2 5.7 %all-to-all-start.1 = ((bf16[8,192,256]{2,1,0:T(8,128)(2,1)}), bf16[8,192,256]{2,1,0:T(8,128)(2,1)S(1)}, u32[]{:S(2)}, u32[]{:S(2)}) async-start(bf16[8,192,256]{2,1,0:T(8,128)(2,1)} %share.1), calls=%async_computation.1 | async-start | bytes 1572864 | tf_op jit(solution)/shard_map/share/all_to_all | solution.py:426
  58.9 0.7 cache.7
  59.7 2.0 %collective-permute-start.5 = (f32[2,32,256]{2,1,0:T(8,128)S(1)}, f32[2,32,256]{2,1,0:T(8,128)S(1)}, u32[]{:S(2)}, u32[]{:S(2)}) collective-permute-start(f32[2,32,256]{2,1,0:T(8,128)S(1)} %get-tuple-element.20), channel_id=1, source_target_pairs={{0,4},{2,6},{4,0},{6,2},{8,12},{10,14},{12,8},{14,10},{1,5},{3,7},... | collective-permute-start | bytes 196616 | tf_op jit(solution)/shard_map/cache/ppermute | solution.py:404
  61.7 4.9 %collective-permute-done.5.other_ref = f32[2,32,256]{2,1,0:T(8,128)S(1)} collective-permute-done((f32[2,32,256]{2,1,0:T(8,128)S(1)}, f32[2,32,256]{2,1,0:T(8,128)S(1)}, u32[]{:S(2)}, u32[]{:S(2)}) %collective-permute-start.5) | collective-permute-done | bytes 65568 | tf_op jit(solution)/shard_map/cache/ppermute | solution.py:404
  66.6 0.7 cache.8
  67.3 1.9 %collective-permute-start.6 = (f32[1,32,256]{2,1,0:T(8,128)S(1)}, f32[1,32,256]{2,1,0:T(8,128)S(1)}, u32[]{:S(2)}, u32[]{:S(2)}) collective-permute-start(f32[1,32,256]{2,1,0:T(8,128)S(1)} %get-tuple-element.22), channel_id=1, source_target_pairs={{0,2},{2,0},{4,6},{6,4},{8,10},{10,8},{12,14},{14,12},{1,3},{3,1},... | collective-permute-start | bytes 98312 | tf_op jit(solution)/shard_map/cache/ppermute | solution.py:404
  69.2 2.7 %collective-permute-done.6.other_ref = f32[1,32,256]{2,1,0:T(8,128)S(1)} collective-permute-done((f32[1,32,256]{2,1,0:T(8,128)S(1)}, f32[1,32,256]{2,1,0:T(8,128)S(1)}, u32[]{:S(2)}, u32[]{:S(2)}) %collective-permute-start.6) | collective-permute-done | bytes 32800 | tf_op jit(solution)/shard_map/cache/ppermute | solution.py:404
  71.9 0.2 cache.9.before.cache_ref
  72.1 5.8 %collective-permute-start.7 = (bf16[1536,256]{1,0:T(8,128)(2,1)S(1)}, bf16[1536,256]{1,0:T(8,128)(2,1)S(1)}, u32[]{:S(2)}, u32[]{:S(2)}) collective-permute-start(bf16[1536,256]{1,0:T(8,128)(2,1)S(1)} %bitcast.9), channel_id=1, source_target_pairs={{0,1},{1,0},{2,3},{3,2},{4,5},{5,4},{6,7},{7,6},{8,9},{9,8},{10,11... | collective-permute-start | bytes 2359304 | tf_op jit(solution)/shard_map/passage_rows/ppermute | solution.py:430
  77.9 1.9 %collective-permute-done.7.other_ref = bf16[1536,256]{1,0:T(8,128)(2,1)S(1)} collective-permute-done((bf16[1536,256]{1,0:T(8,128)(2,1)S(1)}, bf16[1536,256]{1,0:T(8,128)(2,1)S(1)}, u32[]{:S(2)}, u32[]{:S(2)}) %collective-permute-start.7) | collective-permute-done | bytes 786464 | tf_op jit(solution)/shard_map/passage_rows/ppermute | solution.py:430
  79.8 2.1 %passage_rows.1 = f32[4,32,256]{2,1,0:T(8,128)} custom-call(s32[8]{0:T(128)S(1)} %copy-done.4, f32[8,512]{1,0:T(8,128)S(1)} %constant_dynamic-slice_fusion.query_ref, f32[8,512]{1,0:T(8,128)S(1)} %collective-permute-done.1.query1_ref, f32[16,512]{1,0:T(8,128)S(1)} %collective-permute-done.2.before_a.query2_ref, bf16[1536,256]{1,0:T(8,128)(2,1)S(1)} %bitcast.10, ...), custom_call_target="tpu_custom_call" | custom-call | flops 201326592 | bytes 2097152 | tf_op jit(solution)/shard_map/passage_rows/pallas_call | solution.py:332
  81.9 8.3 %all-to-all-start.2 = ((f32[4,32,256]{2,1,0:T(8,128)}), f32[4,32,256]{2,1,0:T(8,128)S(1)}, u32[]{:S(2)}, u32[]{:S(2)}) async-start(f32[4,32,256]{2,1,0:T(8,128)} %passage_rows.1), calls=%async_computation.2 | async-start | bytes 262144 | tf_op jit(solution)/shard_map/passage_rows/all_to_all | solution.py:446
  90.3 11.6 %passage_attention.1 = bf16[384,512]{1,0:T(8,128)(2,1)} custom-call(s32[8]{0:T(128)S(1)} %copy-done.4, bf16[384,512]{1,0:T(8,128)(2,1)S(1)} %bitcast.12, f32[2,384,128]{2,1,0:T(8,128)S(1)} %copy-done.3, f32[2,8,128]{2,1,0:T(8,128)S(1)} %copy-done.5, bf16[1536,256]{1,0:T(8,128)(2,1)S(1)} %bitcast.11, bf16[1536,256]{1,0:T(8,128)(2,1)S(1)} %collective-permute-done.7.other_ref), custom_call_target="tpu_custom_call" | custom-call | flops 9663676416 | bytes 3145728 | tf_op jit(solution)/shard_map/passage_attention/pallas_call | solution.py:332
  101.9 0.8 row_merge.1
  102.7 0.6 reshape.17
  (33 shorter events, 0.2 us)
Async XLA Ops:
  6.3 4.8 %collective-permute-start = (bf16[8,208,256]{2,1,0:T(8,128)(2,1)}, bf16[8,208,256]{2,1,0:T(8,128)(2,1)S(1)}, u32[]{:S(2)}, u32[]{:S(2)}) collective-permute-start(bf16[8,208,256]{2,1,0:T(8,128)(2,1)} %get-tuple-element.14), channel_id=1, source_target_pairs={{0,1},{1,0},{2,3},{3,2},{4,5},{5,4},{6,7},{7,6},{8,9},{9,8},{10,11... | collective-permute-start | bytes 2555912 | tf_op jit(solution)/shard_map/projection/ppermute | solution.py:364
  11.1 1.2 %copy-start = (bf16[8,208,256]{2,1,0:T(8,128)(2,1)S(1)}, bf16[8,208,256]{2,1,0:T(8,128)(2,1)}, u32[]{:S(2)}) copy-start(bf16[8,208,256]{2,1,0:T(8,128)(2,1)} %get-tuple-element.13.mine_ref) | copy-start | bytes 2555908
  13.4 7.0 %copy-start.9 = (bf16[4,2,8192]{2,1,0:T(2,128)(2,1)S(1)}, bf16[4,2,8192]{2,1,0:T(2,128)(2,1)}, u32[]{:S(2)}) copy-start(bf16[4,2,8192]{2,1,0:T(2,128)(2,1)} %param.17) | copy-start | bytes 393220
  13.4 7.0 %copy-start.10 = (bf16[4,2,1024]{2,1,0:T(2,128)(2,1)S(1)}, bf16[4,2,1024]{2,1,0:T(2,128)(2,1)}, u32[]{:S(2)}) copy-start(bf16[4,2,1024]{2,1,0:T(2,128)(2,1)} %param.19) | copy-start | bytes 49156
  13.4 7.0 %copy-start.11 = (bf16[4,2,1024]{2,1,0:T(2,128)(2,1)S(1)}, bf16[4,2,1024]{2,1,0:T(2,128)(2,1)}, u32[]{:S(2)}) copy-start(bf16[4,2,1024]{2,1,0:T(2,128)(2,1)} %param.18) | copy-start | bytes 49156
  13.4 7.2 %copy-start.2 = (bf16[2,128,1024]{2,1,0:T(8,128)(2,1)S(1)}, bf16[2,128,1024]{2,1,0:T(8,128)(2,1)}, u32[]{:S(2)}) copy-start(bf16[2,128,1024]{2,1,0:T(8,128)(2,1)} %value_ref.3) | copy-start | bytes 1572868
  13.4 37.9 %all-to-all-start = ((bf16[8,208,256]{2,1,0:T(8,128)(2,1)}), bf16[8,208,256]{2,1,0:T(8,128)(2,1)S(1)}, u32[]{:S(2)}, u32[]{:S(2)}) async-start(bf16[8,208,256]{2,1,0:T(8,128)(2,1)} %projection.3), calls=%async_computation | async-start | bytes 1703936 | tf_op jit(solution)/shard_map/projection/all_to_all | solution.py:366
  20.4 1.0 %copy-start.1 = (bf16[2,128,1024]{2,1,0:T(8,128)(2,1)S(1)}, bf16[2,128,1024]{2,1,0:T(8,128)(2,1)}, u32[]{:S(2)}) copy-start(bf16[2,128,1024]{2,1,0:T(8,128)(2,1)} %key_ref.3) | copy-start | bytes 1572868
  20.5 0.9 copy-start.4
  20.5 0.9 copy-start.6
  24.1 27.2 %copy-start.3 = (f32[2,384,128]{2,1,0:T(8,128)S(1)}, f32[2,384,128]{2,1,0:T(8,128)}, u32[]{:S(2)}) copy-start(f32[2,384,128]{2,1,0:T(8,128)} %constant.31.clone.near_ref) | copy-start | bytes 1179652
  24.1 8.5 %collective-permute-start.3 = (f32[8,32,256]{2,1,0:T(8,128)S(1)}, f32[8,32,256]{2,1,0:T(8,128)S(1)}, u32[]{:S(2)}, u32[]{:S(2)}) collective-permute-start(f32[8,32,256]{2,1,0:T(8,128)S(1)} %get-tuple-element.16), channel_id=1, source_target_pairs={{0,1},{1,0},{2,3},{3,2},{4,5},{5,4},{6,7},{7,6},{8,9},{9,8},{10,11... | collective-permute-start | bytes 786440 | tf_op jit(solution)/shard_map/cache/ppermute | solution.py:391
  26.9 14.3 %collective-permute-start.1 = (f32[8,512]{1,0:T(8,128)S(1)}, f32[8,512]{1,0:T(8,128)S(1)}, u32[]{:S(2)}, u32[]{:S(2)}) collective-permute-start(f32[8,512]{1,0:T(8,128)S(1)} %constant_dynamic-slice_fusion.query_ref), channel_id=1, source_target_pairs={{0,128},{128,0},{256,384},{384,256},{1,129},{129,1},{257,385},{385... | collective-permute-start | bytes 49160 | tf_op jit(solution)/shard_map/decode_query_exchange/ppermute | solution.py:371
  33.6 17.7 %copy-start.5 = (f32[2,8,128]{2,1,0:T(8,128)S(1)}, f32[2,8,128]{2,1,0:T(8,128)}, u32[]{:S(2)}) copy-start(f32[2,8,128]{2,1,0:T(8,128)} %constant.32.clone.far_ref) | copy-start | bytes 24580
  33.6 17.7 %collective-permute-start.4 = (f32[4,32,256]{2,1,0:T(8,128)S(1)}, f32[4,32,256]{2,1,0:T(8,128)S(1)}, u32[]{:S(2)}, u32[]{:S(2)}) collective-permute-start(f32[4,32,256]{2,1,0:T(8,128)S(1)} %get-tuple-element.17), channel_id=1, source_target_pairs={{0,8},{2,10},{4,12},{6,14},{8,0},{10,2},{12,4},{14,6},{1,9},{3,11}... | collective-permute-start | bytes 393224 | tf_op jit(solution)/shard_map/cache/ppermute | solution.py:404
  41.2 10.1 %collective-permute-start.2 = (f32[16,512]{1,0:T(8,128)S(1)}, f32[16,512]{1,0:T(8,128)S(1)}, u32[]{:S(2)}, u32[]{:S(2)}) collective-permute-start(f32[16,512]{1,0:T(8,128)S(1)} %pad_maximum_fusion), channel_id=1, source_target_pairs={{0,256},{128,384},{256,0},{384,128},{1,257},{129,385},{257,1},{385... | collective-permute-start | bytes 98312 | tf_op jit(solution)/shard_map/decode_query_exchange/ppermute | solution.py:372
  53.2 18.9 %all-to-all-start.1 = ((bf16[8,192,256]{2,1,0:T(8,128)(2,1)}), bf16[8,192,256]{2,1,0:T(8,128)(2,1)S(1)}, u32[]{:S(2)}, u32[]{:S(2)}) async-start(bf16[8,192,256]{2,1,0:T(8,128)(2,1)} %share.1), calls=%async_computation.1 | async-start | bytes 1572864 | tf_op jit(solution)/shard_map/share/all_to_all | solution.py:426
  59.7 6.9 %collective-permute-start.5 = (f32[2,32,256]{2,1,0:T(8,128)S(1)}, f32[2,32,256]{2,1,0:T(8,128)S(1)}, u32[]{:S(2)}, u32[]{:S(2)}) collective-permute-start(f32[2,32,256]{2,1,0:T(8,128)S(1)} %get-tuple-element.20), channel_id=1, source_target_pairs={{0,4},{2,6},{4,0},{6,2},{8,12},{10,14},{12,8},{14,10},{1,5},{3,7},... | collective-permute-start | bytes 196616 | tf_op jit(solution)/shard_map/cache/ppermute | solution.py:404
  67.3 4.7 %collective-permute-start.6 = (f32[1,32,256]{2,1,0:T(8,128)S(1)}, f32[1,32,256]{2,1,0:T(8,128)S(1)}, u32[]{:S(2)}, u32[]{:S(2)}) collective-permute-start(f32[1,32,256]{2,1,0:T(8,128)S(1)} %get-tuple-element.22), channel_id=1, source_target_pairs={{0,2},{2,0},{4,6},{6,4},{8,10},{10,8},{12,14},{14,12},{1,3},{3,1},... | collective-permute-start | bytes 98312 | tf_op jit(solution)/shard_map/cache/ppermute | solution.py:404
  72.1 18.2 %copy-start.8 = (bf16[1,384,512]{2,1,0:T(8,128)(2,1)S(1)}, bf16[1,384,512]{2,1,0:T(8,128)(2,1)}, u32[]{:S(2)}) copy-start(bf16[1,384,512]{2,1,0:T(8,128)(2,1)} %param.14) | copy-start | bytes 1179652
  72.1 7.7 %collective-permute-start.7 = (bf16[1536,256]{1,0:T(8,128)(2,1)S(1)}, bf16[1536,256]{1,0:T(8,128)(2,1)S(1)}, u32[]{:S(2)}, u32[]{:S(2)}) collective-permute-start(bf16[1536,256]{1,0:T(8,128)(2,1)S(1)} %bitcast.9), channel_id=1, source_target_pairs={{0,1},{1,0},{2,3},{3,2},{4,5},{5,4},{6,7},{7,6},{8,9},{9,8},{10,11... | collective-permute-start | bytes 2359304 | tf_op jit(solution)/shard_map/passage_rows/ppermute | solution.py:430
  81.9 20.0 %all-to-all-start.2 = ((f32[4,32,256]{2,1,0:T(8,128)}), f32[4,32,256]{2,1,0:T(8,128)S(1)}, u32[]{:S(2)}, u32[]{:S(2)}) async-start(f32[4,32,256]{2,1,0:T(8,128)} %passage_rows.1), calls=%async_computation.2 | async-start | bytes 262144 | tf_op jit(solution)/shard_map/passage_rows/all_to_all | solution.py:446
  90.3 11.6 %copy-start.7 = (s32[2]{0:T(128)S(1)}, s32[2]{0:T(128)}, u32[]{:S(2)}) copy-start(s32[2]{0:T(128)} %passage_ref.1) | copy-start | bytes 28

commit v3 on v2

v3 whole, which is shorter than its diff:
```python
import functools

import jax
import jax.numpy as jnp
import numpy as np
from jax import lax
from jax.experimental import pallas as pl
from jax.experimental.pallas import tpu as pltpu
from jax.sharding import Mesh
from jax.sharding import PartitionSpec as P

D = 8192
KVH = 8
HS = 128
SEQ = 8
TOK = 384
HALF = 192
HEADS = 4
EXTRA = 16
KV_ROWS = HALF + EXTRA
ROWS = KV_ROWS + 32
ROPE_BASE = 500000.0
NORM_EPS = 1e-05
NEG = -1e30
SCALE2 = float(HS**-0.5 * np.log2(np.e))

bf16, f32 = jnp.bfloat16, jnp.float32
dot = functools.partial(jnp.dot, preferred_element_type=f32)


def dot_t(a, b):
    return lax.dot_general(a, b, (((1,), (1,)), ((), ())), preferred_element_type=f32)


def tables():
    freq = ROPE_BASE ** (-(np.arange(HS // 2) * 2.0 / HS))
    freq = np.concatenate([freq, freq])
    near = np.arange(TOK)[:, None] * freq
    far = (np.arange(SEQ) * TOK)[:, None] * freq
    near = np.stack([np.cos(near), np.sin(near)]).astype(np.float32)
    far = np.stack([np.cos(far), np.sin(far)]).astype(np.float32)
    return near, far


def turn_by(near_ref, far_ref, s, rows):
    cn, sn = near_ref[0, rows, :], near_ref[1, rows, :]
    cf, sf = far_ref[0, pl.ds(s, 1), :], far_ref[1, pl.ds(s, 1), :]
    cosine = cn * cf - sn * sf
    sine = sn * cf + cn * sf
    lane = lax.broadcasted_iota(jnp.int32, sine.shape, 1)
    return cosine, jnp.where(lane < HS // 2, -sine, sine)


def turned(x, cosine, sine):
    return x * cosine + pltpu.roll(x, HS // 2, 1) * sine


def project(hidden_ref, key_ref, value_ref, mine_ref, theirs_ref, squares_ref, rows_ref):
    core = lax.axis_index("core")

    @pl.when(pl.program_id(0) == 0)
    def _():
        for half, at in enumerate((core, 1 - core)):
            rows = pl.ds(pl.multiple_of(at * HALF, HALF), HALF)
            rows_ref[half * HALF : (half + 1) * HALF] = hidden_ref[rows, :]
        h = rows_ref[...].astype(f32)
        squares = jnp.broadcast_to(jnp.sum(h * h, axis=1, keepdims=True), (TOK, HS))
        squares = jnp.transpose(squares)[:EXTRA]
        row = lax.broadcasted_iota(jnp.int32, (EXTRA, 256), 0)
        tp = lax.axis_index("y") * 2 + core
        for half in range(2):
            part = squares[:, half * HALF : (half + 1) * HALF]
            part = jnp.concatenate([part, jnp.zeros((EXTRA, 256 - HALF), f32)], axis=1)
            squares_ref[half] = jnp.where(row == tp, part, 0.0).astype(bf16)

    h = rows_ref[...]
    for half, out_ref in enumerate((mine_ref, theirs_ref)):
        for j in range(out_ref.shape[0]):
            out_ref[j, HALF:, :] = squares_ref[half]
    for at, weight_ref in ((0, key_ref), (HS, value_ref)):
        for j in range(0, mine_ref.shape[0], 2):
            both = dot(h, weight_ref[:, j * HS : (j + 2) * HS]).astype(bf16)
            for half, out_ref in enumerate((mine_ref, theirs_ref)):
                part = both[half * HALF : (half + 1) * HALF]
                out_ref[j, :HALF, at : at + HS] = part[:, :HS]
                out_ref[j + 1, :HALF, at : at + HS] = part[:, HS:]


def add(mine_ref, other_ref, cache_ref, tail_ref, out_ref):
    total = mine_ref[...].astype(f32) + other_ref[...].astype(f32)
    out_ref[:, :HALF, :] = total[:, :HALF, :].astype(bf16)
    out_ref[:, HALF:KV_ROWS, :] = (total[:, HALF:, :] + tail_ref[...].astype(f32)).astype(bf16)
    out_ref[:, KV_ROWS:, :] = cache_ref[...]


def finish_share(sums_ref, near_ref, far_ref, out_ref, keep_ref, send_ref):
    s, core = lax.axis_index("seq"), lax.axis_index("core")
    count = sums_ref.shape[0]
    squares, sums, highs, totals = 0.0, 0.0, [], []
    for k in range(count):
        sums = sums + sums_ref[k, :HALF, :].astype(f32)
        extra = sums_ref[k, HALF:KV_ROWS, :].astype(f32)
        squares = squares + extra
        highs.append(extra[0:1, HALF:] + extra[1:2, HALF:] + extra[2:3, HALF:])
        totals.append(extra[3:4, HALF:] + extra[4:5, HALF:] + extra[5:6, HALF:])
    highest = functools.reduce(jnp.maximum, highs)
    factors = [jnp.exp2(high - highest) for high in highs]
    total = sum(f * t for f, t in zip(factors, totals, strict=True))
    rows = lax.broadcasted_iota(jnp.int32, (EXTRA, 256 - HALF), 0)
    table = 0.0
    for i, row in enumerate([*factors, highest, total]):
        table = jnp.where(rows == i, row, table)
    table = jnp.concatenate([table, jnp.zeros((EXTRA, HALF - HS), f32)], axis=1)
    table = jnp.transpose(table)[: 256 - HALF, :]
    weighted = 0.0
    for k in range(count):
        both = sums_ref[k, KV_ROWS:, :].astype(f32)
        both = jnp.concatenate([both[:, :HS], both[:, HS:]], axis=0)
        weighted = weighted + both * table[:, k : k + 1]
    state = state_of(weighted, table[:, count : count + 1], table[:, count + 1 : count + 2])
    keep_ref[...] = jnp.where(core == 0, state[:32], state[32:])
    send_ref[...] = jnp.where(core == 0, state[32:], state[:32])
    squares = jnp.sum(squares, axis=0, keepdims=True)
    inverse = lax.rsqrt(squares * (1.0 / D) + NORM_EPS)
    inverse = jnp.transpose(jnp.broadcast_to(inverse, (8, 256)))[:HALF, 0:1]
    alive = inverse > 0.0
    scaled = jnp.where(alive, sums * inverse, 0.0)
    rows = pl.ds(pl.multiple_of(core * HALF, HALF), HALF)
    cosine, sine = turn_by(near_ref, far_ref, s, rows)
    keys = turned(scaled[:, :HS], cosine, sine)
    share = jnp.concatenate([keys, scaled[:, HS:]], axis=1).astype(bf16)
    for to in range(SEQ):
        out_ref[to] = share


def state_of(weighted, highest, totals):
    lane = lax.broadcasted_iota(jnp.int32, weighted.shape, weighted.ndim - 1)
    tail = jnp.where(lane < HS // 2, highest, totals)
    return jnp.concatenate([weighted, tail], axis=-1)


def parts_of(state):
    return state[..., :HS], state[..., HS : HS + 1], state[..., HS + HS // 2 : HS + HS // 2 + 1]


def merged(a, b):
    (a_sum, a_high, a_total), (b_sum, b_high, b_total) = parts_of(a), parts_of(b)
    highest = jnp.maximum(a_high, b_high)
    a_factor, b_factor = jnp.exp2(a_high - highest), jnp.exp2(b_high - highest)
    return state_of(
        a_sum * a_factor + b_sum * b_factor, highest, a_total * a_factor + b_total * b_factor
    )


def pieces(x):
    first = x.astype(bf16).astype(f32)
    second = (x - first).astype(bf16).astype(f32)
    return first, second, x - first - second


def cache_states(
    length_ref, passage_ref, query_ref, new_ref, key_ref, value_ref, sum_ref, tail_ref, chosen_ref
):
    tp = lax.axis_index("y") * 2 + lax.axis_index("core")
    slots = key_ref.shape[1]
    rows, keys = KVH * 64, 2 * slots + 16
    row = lax.broadcasted_iota(jnp.int32, chosen_ref.shape, 0) & 1
    chosen_ref[...] = jnp.where(row == 1, passage_ref[1], passage_ref[0])

    q = lax.broadcasted_iota(jnp.int32, (64, keys), 0)
    n = lax.broadcasted_iota(jnp.int32, (64, keys), 1)
    key_row = jnp.where(n >= slots, 1, 0)
    slot = tp * slots + n - key_row * slots
    length = jnp.where(key_row == 1, length_ref[1], length_ref[0])
    live = ((q & 1) == key_row) & (slot < length) & (n < 2 * slots)
    new = n - 2 * slots
    recent = ((q & 1) == (new & 1)) & ((new >> 1) <= ((q & 7) >> 1)) & (tp == 0)
    live = live | (recent & (new >= 0) & (new < 8))
    live = jnp.where(live, 1.0, 0.0)
    live = jnp.concatenate([live] * KVH, axis=0) > 0.5

    news = jnp.concatenate([new_ref[...], jnp.zeros(new_ref.shape, f32)], axis=0).astype(bf16)
    scores = []
    for head in range(KVH):
        cols = slice(head * HS, (head + 1) * HS)
        query = jnp.concatenate(
            [query_ref[:, (head * 8 + p) * HS : (head * 8 + p + 1) * HS] for p in range(8)], axis=0
        ).astype(bf16)
        every = jnp.concatenate([key_ref[0, :, cols], key_ref[1, :, cols], news[:, cols]], axis=0)
        scores.append(dot_t(query, every))
    scores = jnp.where(live, jnp.concatenate(scores, axis=0) * SCALE2, NEG)
    highest = jnp.max(scores, axis=1, keepdims=True)
    weights = jnp.where(live, jnp.exp2(scores - highest), 0.0)
    totals = jnp.sum(weights, axis=1, keepdims=True)
    weights = weights.astype(bf16)
    lane = lax.broadcasted_iota(jnp.int32, (rows, HS), 1)
    tail = 0.0
    for i, piece in enumerate(pieces(highest) + pieces(totals)):
        tail = jnp.where(lane == i, piece, tail)
    tail = jnp.transpose(tail)[:EXTRA, :]
    for head in range(KVH):
        cols = slice(head * HS, (head + 1) * HS)
        part = slice(head * 64, (head + 1) * 64)
        late = slice((KVH + head) * HS, (KVH + head + 1) * HS)
        every = jnp.concatenate(
            [value_ref[0, :, cols], value_ref[1, :, cols], news[:, late]], axis=0
        )
        weighted = dot(weights[part], every)
        sum_ref[head] = jnp.concatenate([weighted[:32], weighted[32:]], axis=1).astype(bf16)
        tail_ref[head] = jnp.concatenate(
            [jnp.zeros((EXTRA, HALF), f32), tail[:, part]], axis=1
        ).astype(bf16)


def passage_states(
    query_ref, query1_ref, query2_ref, own_ref, other_ref, out_ref
):
    queries = [query_ref[...], query1_ref[...], query2_ref[:8, :], query2_ref[8:, :]]
    query = jnp.concatenate(
        [rows[:, p * HS : (p + 1) * HS] for rows in queries for p in range(HEADS)], axis=0
    ).astype(bf16)
    refs = (own_ref, other_ref)
    scores = [dot_t(query, ref[:, :HS]) * SCALE2 for ref in refs]
    highest = jnp.max(jnp.maximum(*scores), axis=1, keepdims=True)
    weights = [jnp.exp2(score - highest) for score in scores]
    totals = jnp.sum(weights[0] + weights[1], axis=1, keepdims=True)
    weighted = sum(dot(w.astype(bf16), ref[:, HS:]) for w, ref in zip(weights, refs, strict=True))
    state = state_of(weighted, highest, totals)
    for r in range(4):
        out_ref[lax.axis_index("group") ^ r] = state[32 * r : 32 * (r + 1)]


def attend(query_ref, near_ref, far_ref, own_ref, other_ref, out_ref, turned_ref, values_ref):
    s, core = lax.axis_index("seq"), lax.axis_index("core")
    cosine, sine = turn_by(near_ref, far_ref, s, slice(None))
    cosine, sine = cosine * SCALE2, sine * SCALE2
    for h in range(HEADS):
        x = query_ref[:, h * HS : (h + 1) * HS].astype(f32)
        turned_ref[h] = turned(x, cosine, sine).astype(bf16)

    def run(pairs):
        keys = pairs * TOK
        early, late = slice(0, keys - TOK), slice(keys - TOK, keys)
        for c, ref in enumerate((own_ref, other_ref)):
            values_ref[c, :keys, :HS] = ref[:keys, HS:]
            values_ref[c, :keys, HS:] = jnp.ones((keys, HS), bf16)
        n = lax.broadcasted_iota(jnp.int32, (1, TOK), 1)
        second = jnp.where(n >= HALF, 1, 0)
        key_pos = (2 * (pairs - 1) + second) * TOK + n - second * HALF
        query_pos = s * TOK + lax.broadcasted_iota(jnp.int32, (TOK, 1), 0)

        def head(h, carry):
            query = turned_ref[h]
            scores, values = [], []
            for c, ref in enumerate((own_ref, other_ref)):
                if pairs > 1:
                    scores.append(dot_t(query, ref[early, :HS]))
                    values.append(values_ref[c, early, :])
                offset = core * HALF if c == 0 else (1 - core) * HALF
                score = dot_t(query, ref[late, :HS])
                scores.append(jnp.where(key_pos + offset <= query_pos, score, NEG))
                values.append(values_ref[c, late, :])
            highest = functools.reduce(
                jnp.maximum, [jnp.max(score, axis=1, keepdims=True) for score in scores]
            )
            total = 0.0
            for score, value in zip(scores, values, strict=True):
                total = total + dot(jnp.exp2(score - highest).astype(bf16), value)
            context = (total[:, :HS] / total[:, HS : HS + 1]).astype(bf16)
            out_ref[:, pl.ds(pl.multiple_of(h * HS, HS), HS)] = context
            return carry

        lax.fori_loop(0, HEADS, head, 0, unroll=2)

    for pairs in range(1, SEQ // 2 + 1):
        pl.when(s // 2 == pairs - 1)(functools.partial(run, pairs))


def merge(chosen_ref, passages_ref, cache_ref, other_ref, out_ref):
    chosen = chosen_ref[...]
    state = passages_ref[0]
    for g in range(1, passages_ref.shape[0]):
        state = jnp.where(chosen == g, passages_ref[g], state)
    weighted, _, total = parts_of(merged(state, merged(cache_ref[...], other_ref[...])))
    context = weighted / total
    for step in range(out_ref.shape[0]):
        for p in range(HEADS):
            rows = context[p * 8 + 2 * step : p * 8 + 2 * step + 2, :]
            out_ref[step, :, p * HS : (p + 1) * HS] = rows.astype(bf16)


def vmem(count):
    return [pl.BlockSpec(memory_space=pltpu.VMEM)] * count


def smem(count):
    return [pl.BlockSpec(memory_space=pltpu.SMEM)] * count


def params(mib):
    return pltpu.CompilerParams(vmem_limit_bytes=mib << 20)


def cost(flops, transcendentals=0, bytes_accessed=1 << 20):
    return pl.CostEstimate(
        flops=flops, transcendentals=transcendentals, bytes_accessed=bytes_accessed
    )


def per_device(
    hidden,
    passage_queries,
    key_weight,
    value_weight,
    decode_queries,
    new_keys,
    new_values,
    cache_keys,
    cache_values,
    cache_lengths,
    passage_of_row,
):
    near, far = tables()
    groups = lax.axis_size("group")
    tp = lax.axis_index("y") * 2 + lax.axis_index("core")
    features = hidden.shape[2]
    swap = [(0, 1), (1, 0)]
    state = (32, 2 * HS)

    def call(kernel, out, scalars, arrays, *operands, mib=32, **more):
        single = not isinstance(out, list)
        result = pl.pallas_call(
            kernel,
            in_specs=smem(scalars) + vmem(arrays),
            out_specs=vmem(1 if single else len(out)),
            out_shape=[out] if single else out,
            compiler_params=params(mib),
            **more,
        )(*operands)
        return result[0] if single else result

    shape = jax.ShapeDtypeStruct

    with jax.named_scope("projection"):
        width = 4
        block = pl.BlockSpec((width, HALF + EXTRA, 2 * HS), lambda i: (i, 0, 0))
        chunk = shape((KVH, HALF + EXTRA, 2 * HS), bf16)
        mine, theirs = pl.pallas_call(
            project,
            grid=(KVH // width,),
            in_specs=[
                pl.BlockSpec((TOK, features), lambda i: (0, 0)),
                pl.BlockSpec((features, width * HS), lambda i: (0, i)),
                pl.BlockSpec((features, width * HS), lambda i: (0, i)),
            ],
            out_specs=[block, block],
            out_shape=[chunk, chunk],
            scratch_shapes=[
                pltpu.VMEM((2, EXTRA, 256), bf16),
                pltpu.VMEM((TOK, features), bf16),
            ],
            compiler_params=params(56),
            cost_estimate=cost(2 * TOK * features * 2048, 0, 4 << 20),
        )(hidden[0], key_weight, value_weight)
        theirs = lax.ppermute(theirs, "core", swap)

    with jax.named_scope("cache"):
        queries = decode_queries.reshape(8, -1).astype(f32)
        news = jnp.concatenate([new_keys, new_values], axis=2).reshape(8, -1).astype(f32)
        cache_sums, cache_tails, chosen = call(
            cache_states,
            [
                shape((KVH, 32, 2 * HS), bf16),
                shape((KVH, EXTRA, 2 * HS), bf16),
                shape(state, jnp.int32),
            ],
            2,
            4,
            cache_lengths,
            passage_of_row,
            queries,
            news,
            cache_keys,
            cache_values,
            cost_estimate=cost(8 * 64 * 256 * 128 * 4, 8 * 64 * 256, 2 << 20),
        )

    with jax.named_scope("sums"):
        chunks = call(
            add,
            shape((KVH, ROWS, 2 * HS), bf16),
            0,
            4,
            mine,
            theirs,
            cache_sums,
            cache_tails,
            cost_estimate=cost(1 << 20),
        )
        sums = lax.all_to_all(chunks, "y", 0, 0, tiled=True)

    with jax.named_scope("decode_query_exchange"):
        queries, _ = lax.optimization_barrier((queries, chunks))
        own = lax.dynamic_slice_in_dim(queries, tp * HEADS * HS, HEADS * HS, 1)
        near_group = lax.ppermute(own, "group", [(g, g ^ 1) for g in range(groups)])
        far_groups = lax.ppermute(
            jnp.concatenate([own, near_group]), "group", [(g, g ^ 2) for g in range(groups)]
        )

    with jax.named_scope("share"):
        sums, far_groups = lax.optimization_barrier((sums, far_groups))
        share, keep, send = call(
            finish_share,
            [shape((SEQ, HALF, 2 * HS), bf16), shape(state, f32), shape(state, f32)],
            0,
            3,
            sums,
            near,
            far,
            cost_estimate=cost(1 << 20),
        )
        received = lax.all_to_all(share, "seq", 0, 0, tiled=True)
        other = lax.ppermute(send, "core", swap)

    with jax.named_scope("passage_rows"):
        own_kv, _ = lax.optimization_barrier((received.reshape(SEQ * HALF, 2 * HS), other))
        other_kv = lax.ppermute(own_kv, "core", swap)
        rows_passage = call(
            passage_states,
            shape((groups, *state), f32),
            0,
            5,
            own,
            near_group,
            far_groups,
            own_kv,
            other_kv,
            cost_estimate=cost(128 * 3072 * 128 * 4, 128 * 3072, 2 << 20),
        )
        returned = lax.all_to_all(rows_passage, "group", 0, 0, tiled=True)

    with jax.named_scope("passage_attention"):
        passage_out = call(
            attend,
            shape((TOK, HEADS * HS), bf16),
            0,
            5,
            passage_queries[0],
            near,
            far,
            own_kv,
            other_kv,
            mib=48,
            scratch_shapes=[
                pltpu.VMEM((HEADS, TOK, HS), bf16),
                pltpu.VMEM((2, SEQ * HALF, 2 * HS), bf16),
            ],
            cost_estimate=cost(1536 * 3072 * 128 * 4 * 4, 1536 * 3072, 3 << 20),
        )

    with jax.named_scope("row_merge"):
        row_out = call(
            merge,
            shape((4, 2, HEADS * HS), bf16),
            0,
            4,
            chosen,
            returned,
            keep,
            other,
            cost_estimate=cost(1 << 20),
        )
    return passage_out[None], row_out


def solution(mesh):
    shape = tuple(mesh.shape[name] for name in ("group", "seq", "tp"))
    split = Mesh(
        mesh.devices.reshape(shape[0], shape[1], shape[2] // 2, 2), ("group", "seq", "y", "core")
    )
    tp, rows = ("y", "core"), ("group", "seq")
    in_specs = (
        P("group", "seq", tp),
        P("group", "seq", tp),
        P(tp, None),
        P(tp, None),
        P(None, rows, None),
        P(None, rows, None),
        P(None, rows, None),
        P(rows, tp, None),
        P(rows, tp, None),
        P(rows),
        P(rows),
    )
    out_specs = (P("group", "seq", tp), P(None, rows, tp))
    return jax.shard_map(
        per_device, mesh=split, in_specs=in_specs, out_specs=out_specs, check_vma=False
    )
```

time: 104 us -> 90.9 us (0.87)
  the two profiles are of different devices: /device:TPU:7 before, /device:TPU:1 now
where the time goes in v3:
time: 90.9 us; the launch traced here: 90.3 us
  starting transfers between devices  46.6 us (51%)
  waiting for transfers between devices  28.1 us (31%)
  Pallas kernels  14.2 us (16%)
    pallas_call x6, Pallas kernels, call(): pl.pallas_call(kernel, in_specs=smem(scalars) + vmem(arrays), out_specs=v...  10.3 us
    all_to_all x1, waiting for transfers between devices, per_device(): sums = lax.all_to_all(chunks, 'y', 0, 0, tiled=True)  10.2 us
    all_to_all x1, starting transfers between devices, per_device(): returned = lax.all_to_all(rows_passage, 'group', 0, 0, tiled=True)  9.12 us
    ppermute x1, starting transfers between devices, per_device(): theirs = lax.ppermute(theirs, 'core', swap)  8.91 us
    ppermute x1, starting transfers between devices, per_device(): lax.ppermute(jnp.concatenate([own, near_group]), 'group', [(g, g ^ 2) for...  8.49 us
    all_to_all x1, waiting for transfers between devices, per_device(): received = lax.all_to_all(share, 'seq', 0, 0, tiled=True)  8.37 us
    all_to_all x1, starting transfers between devices, per_device(): received = lax.all_to_all(share, 'seq', 0, 0, tiled=True)  6.07 us
    ppermute x1, starting transfers between devices, per_device(): other_kv = lax.ppermute(own_kv, 'core', swap)  3.99 us
  transfers between devices with their start and end apart: 8, of which 8 were waited for; matrix products, arithmetic and copies ran while one was open for 0% of the time, Pallas kernels for 6%

profile of v3, /device:TPU:1, one launch (start us, length us, event | category | flops | bytes accessed | tf_op | source)
XLA Modules:
  0.0 90.3 jit_solution(1670939849785029216)
XLA Ops:
  0.6 0.0 copy-start.8
  0.6 0.0 copy-start.9
  0.7 0.0 copy-start.10
  0.7 0.0 copy-start.2
  0.7 3.9 %projection.1 = (bf16[8,208,256]{2,1,0:T(8,128)(2,1)}, bf16[8,208,256]{2,1,0:T(8,128)(2,1)}) custom-call(bf16[384,512]{1,0:T(8,128)(2,1)} %bitcast.8, bf16[512,1024]{1,0:T(8,128)(2,1)} %key_ref.2, bf16[512,1024]{1,0:T(8,128)(2,1)} %value_ref.2), custom_call_target="tpu_custom_call" | custom-call | flops 805306368 | bytes 4194304 | tf_op jit(solution)/shard_map/projection/pallas_call | solution.py:348
  4.6 8.9 %collective-permute-start = (bf16[8,208,256]{2,1,0:T(8,128)(2,1)}, bf16[8,208,256]{2,1,0:T(8,128)(2,1)S(1)}, u32[]{:S(2)}, u32[]{:S(2)}) collective-permute-start(bf16[8,208,256]{2,1,0:T(8,128)(2,1)} %get-tuple-element.15), channel_id=1, source_target_pairs={{0,1},{1,0},{2,3},{3,2},{4,5},{5,4},{6,7},{7,6},{8,9},{9,8},{10,11... | collective-permute-start | bytes 2555912 | tf_op jit(solution)/shard_map/projection/ppermute | solution.py:365
  13.5 0.0 copy-start.5
  13.5 0.0 copy-start.6
  13.7 0.4 copy-done.5
  14.1 0.0 copy-done.6
  14.2 1.4 %cache.1 = (bf16[8,32,256]{2,1,0:T(8,128)(2,1)S(1)}, bf16[8,16,256]{2,1,0:T(8,128)(2,1)S(1)}, s32[32,256]{1,0:T(8,128)S(1)}) custom-call(s32[2]{0:T(128)S(1)} %copy-done.5, s32[2]{0:T(128)S(1)} %copy-done.6, f32[8,8192]{1,0:T(8,128)S(1)} %reshape.14.query_ref, f32[8,2048]{1,0:T(8,128)S(1)} %reshape.15.new_ref, bf16[2,128,1024]{2,1,0:T(8,128)(2,1)S(1)} %copy-done.1, ...), custom_call_target="tpu_custom_call" | custom-call | flops 67108864 | bytes 2097152 | tf_op jit(solution)/shard_map/cache/pallas_call | solution.py:332
  15.5 0.1 collective-permute-done.other_ref
  15.7 1.2 %sums.1 = bf16[8,240,256]{2,1,0:T(8,128)(2,1)} custom-call(bf16[8,208,256]{2,1,0:T(8,128)(2,1)S(1)} %copy-done, bf16[8,208,256]{2,1,0:T(8,128)(2,1)S(1)} %collective-permute-done.other_ref, bf16[8,32,256]{2,1,0:T(8,128)(2,1)S(1)} %get-tuple-element.16.cache_ref, bf16[8,16,256]{2,1,0:T(8,128)(2,1)S(1)} %get-tuple-element.17.tail_ref), custom_call_target="tpu_custom_call" | custom-call | flops 1048576 | bytes 1048576 | tf_op jit(solution)/shard_map/sums/pallas_call | solution.py:332
  16.9 3.7 %all-to-all-start = ((bf16[8,240,256]{2,1,0:T(8,128)(2,1)}), bf16[8,240,256]{2,1,0:T(8,128)(2,1)S(1)}, u32[]{:S(2)}, u32[]{:S(2)}) async-start(bf16[8,240,256]{2,1,0:T(8,128)(2,1)} %sums.1), calls=%async_computation | async-start | bytes 1966080 | tf_op jit(solution)/shard_map/sums/all_to_all | solution.py:400
  20.6 0.0 copy-start.4
  20.6 3.7 %collective-permute-start.1 = (f32[8,512]{1,0:T(8,128)S(1)}, f32[8,512]{1,0:T(8,128)S(1)}, u32[]{:S(2)}, u32[]{:S(2)}) collective-permute-start(f32[8,512]{1,0:T(8,128)S(1)} %constant_dynamic-slice_fusion.query_ref), channel_id=1, source_target_pairs={{0,128},{128,0},{256,384},{384,256},{1,129},{129,1},{257,385},{385... | collective-permute-start | bytes 49160 | tf_op jit(solution)/shard_map/decode_query_exchange/ppermute | solution.py:405
  24.3 1.7 %collective-permute-done.1.query1_ref = f32[8,512]{1,0:T(8,128)S(1)} collective-permute-done((f32[8,512]{1,0:T(8,128)S(1)}, f32[8,512]{1,0:T(8,128)S(1)}, u32[]{:S(2)}, u32[]{:S(2)}) %collective-permute-start.1) | collective-permute-done | bytes 16416 | tf_op jit(solution)/shard_map/decode_query_exchange/ppermute | solution.py:405
  26.0 8.5 %collective-permute-start.2 = (f32[16,512]{1,0:T(8,128)S(1)}, f32[16,512]{1,0:T(8,128)S(1)}, u32[]{:S(2)}, u32[]{:S(2)}) collective-permute-start(f32[16,512]{1,0:T(8,128)S(1)} %pad_maximum_fusion), channel_id=1, source_target_pairs={{0,256},{128,384},{256,0},{384,128},{1,257},{129,385},{257,1},{385... | collective-permute-start | bytes 98312 | tf_op jit(solution)/shard_map/decode_query_exchange/ppermute | solution.py:406
  34.5 1.3 %collective-permute-done.2.query2_ref = f32[16,512]{1,0:T(8,128)S(1)} collective-permute-done((f32[16,512]{1,0:T(8,128)S(1)}, f32[16,512]{1,0:T(8,128)S(1)}, u32[]{:S(2)}, u32[]{:S(2)}) %collective-permute-start.2) | collective-permute-done | bytes 32800 | tf_op jit(solution)/shard_map/decode_query_exchange/ppermute | solution.py:406
  35.8 10.2 %all-to-all-done.sums_ref = bf16[8,240,256]{2,1,0:T(8,128)(2,1)S(1)} async-done(((bf16[8,240,256]{2,1,0:T(8,128)(2,1)}), bf16[8,240,256]{2,1,0:T(8,128)(2,1)S(1)}, u32[]{:S(2)}, u32[]{:S(2)}) %all-to-all-start) | async-done | bytes 983072 | tf_op jit(solution)/shard_map/sums/all_to_all | solution.py:400
  46.0 1.4 %share.1 = (bf16[8,192,256]{2,1,0:T(8,128)(2,1)}, f32[32,256]{1,0:T(8,128)S(1)}, f32[32,256]{1,0:T(8,128)S(1)}) custom-call(bf16[8,240,256]{2,1,0:T(8,128)(2,1)S(1)} %all-to-all-done.sums_ref, f32[2,384,128]{2,1,0:T(8,128)S(1)} %copy-done.3, f32[2,8,128]{2,1,0:T(8,128)S(1)} %copy-done.4), custom_call_target="tpu_custom_call" | custom-call | flops 1048576 | bytes 1048576 | tf_op jit(solution)/shard_map/share/pallas_call | solution.py:332
  47.4 6.1 %all-to-all-start.1 = ((bf16[8,192,256]{2,1,0:T(8,128)(2,1)}), bf16[8,192,256]{2,1,0:T(8,128)(2,1)S(1)}, u32[]{:S(2)}, u32[]{:S(2)}) async-start(bf16[8,192,256]{2,1,0:T(8,128)(2,1)} %get-tuple-element.20), calls=%async_computation.1 | async-start | bytes 1572864 | tf_op jit(solution)/shard_map/share/all_to_all | solution.py:422
  53.5 2.7 %collective-permute-start.3 = (f32[32,256]{1,0:T(8,128)S(1)}, f32[32,256]{1,0:T(8,128)S(1)}, u32[]{:S(2)}, u32[]{:S(2)}) collective-permute-start(f32[32,256]{1,0:T(8,128)S(1)} %get-tuple-element.21), channel_id=1, source_target_pairs={{0,1},{1,0},{2,3},{3,2},{4,5},{5,4},{6,7},{7,6},{8,9},{9,8},{10,11... | collective-permute-start | bytes 98312 | tf_op jit(solution)/shard_map/share/ppermute | solution.py:423
  56.2 0.8 collective-permute-done.3.other_ref
  57.0 8.4 %all-to-all-done.1 = bf16[8,192,256]{2,1,0:T(8,128)(2,1)S(1)} async-done(((bf16[8,192,256]{2,1,0:T(8,128)(2,1)}), bf16[8,192,256]{2,1,0:T(8,128)(2,1)S(1)}, u32[]{:S(2)}, u32[]{:S(2)}) %all-to-all-start.1) | async-done | bytes 786464 | tf_op jit(solution)/shard_map/share/all_to_all | solution.py:422
  65.4 4.0 %collective-permute-start.4 = (bf16[1536,256]{1,0:T(8,128)(2,1)S(1)}, bf16[1536,256]{1,0:T(8,128)(2,1)S(1)}, u32[]{:S(2)}, u32[]{:S(2)}) collective-permute-start(bf16[1536,256]{1,0:T(8,128)(2,1)S(1)} %bitcast.4), channel_id=1, source_target_pairs={{0,1},{1,0},{2,3},{3,2},{4,5},{5,4},{6,7},{7,6},{8,9},{9,8},{10,11... | collective-permute-start | bytes 2359304 | tf_op jit(solution)/shard_map/passage_rows/ppermute | solution.py:427
  69.4 1.9 %collective-permute-done.4.other_ref = bf16[1536,256]{1,0:T(8,128)(2,1)S(1)} collective-permute-done((bf16[1536,256]{1,0:T(8,128)(2,1)S(1)}, bf16[1536,256]{1,0:T(8,128)(2,1)S(1)}, u32[]{:S(2)}, u32[]{:S(2)}) %collective-permute-start.4) | collective-permute-done | bytes 786464 | tf_op jit(solution)/shard_map/passage_rows/ppermute | solution.py:427
  71.3 1.6 %passage_rows.1 = f32[4,32,256]{2,1,0:T(8,128)} custom-call(f32[8,512]{1,0:T(8,128)S(1)} %constant_dynamic-slice_fusion.query_ref, f32[8,512]{1,0:T(8,128)S(1)} %collective-permute-done.1.query1_ref, f32[16,512]{1,0:T(8,128)S(1)} %collective-permute-done.2.query2_ref, bf16[1536,256]{1,0:T(8,128)(2,1)S(1)} %bitcast.5, ...), custom_call_target="tpu_custom_call" | custom-call | flops 201326592 | bytes 2097152 | tf_op jit(solution)/shard_map/passage_rows/pallas_call | solution.py:332
  72.9 9.1 %all-to-all-start.2 = ((f32[4,32,256]{2,1,0:T(8,128)}), f32[4,32,256]{2,1,0:T(8,128)S(1)}, u32[]{:S(2)}, u32[]{:S(2)}) async-start(f32[4,32,256]{2,1,0:T(8,128)} %passage_rows.1), calls=%async_computation.2 | async-start | bytes 262144 | tf_op jit(solution)/shard_map/passage_rows/all_to_all | solution.py:440
  82.0 3.7 %passage_attention.1 = bf16[384,512]{1,0:T(8,128)(2,1)} custom-call(bf16[384,512]{1,0:T(8,128)(2,1)S(1)} %bitcast.7, f32[2,384,128]{2,1,0:T(8,128)S(1)} %copy-done.3, f32[2,8,128]{2,1,0:T(8,128)S(1)} %copy-done.4, bf16[1536,256]{1,0:T(8,128)(2,1)S(1)} %bitcast.6, bf16[1536,256]{1,0:T(8,128)(2,1)S(1)} %collective-permute-done.4.other_ref), custom_call_target="tpu_custom_call" | custom-call | flops 9663676416 | bytes 3145728 | tf_op jit(solution)/shard_map/passage_attention/pallas_call | solution.py:332
  85.7 3.6 %all-to-all-done.2.passages_ref = f32[4,32,256]{2,1,0:T(8,128)S(1)} async-done(((f32[4,32,256]{2,1,0:T(8,128)}), f32[4,32,256]{2,1,0:T(8,128)S(1)}, u32[]{:S(2)}, u32[]{:S(2)}) %all-to-all-start.2) | async-done | bytes 131104 | tf_op jit(solution)/shard_map/passage_rows/all_to_all | solution.py:440
  89.4 1.0 %row_merge.1 = bf16[4,2,512]{2,1,0:T(2,128)(2,1)} custom-call(s32[32,256]{1,0:T(8,128)S(1)} %get-tuple-element.23.chosen_ref, f32[4,32,256]{2,1,0:T(8,128)S(1)} %all-to-all-done.2.passages_ref, f32[32,256]{1,0:T(8,128)S(1)} %get-tuple-element.25.cache_ref, f32[32,256]{1,0:T(8,128)S(1)} %collective-permute-done.3.other_ref), custom_call_target="tpu_custom_call" | custom-call | flops 1048576 | bytes 1048576 | tf_op jit(solution)/shard_map/row_merge/pallas_call | solution.py:332
  (18 shorter events, 0.2 us)
Async XLA Ops:
  0.6 12.9 %copy-start.8 = (bf16[4,2,8192]{2,1,0:T(2,128)(2,1)S(1)}, bf16[4,2,8192]{2,1,0:T(2,128)(2,1)}, u32[]{:S(2)}) copy-start(bf16[4,2,8192]{2,1,0:T(2,128)(2,1)} %param.17) | copy-start | bytes 393220
  0.6 12.9 %copy-start.9 = (bf16[4,2,1024]{2,1,0:T(2,128)(2,1)S(1)}, bf16[4,2,1024]{2,1,0:T(2,128)(2,1)}, u32[]{:S(2)}) copy-start(bf16[4,2,1024]{2,1,0:T(2,128)(2,1)} %param.19) | copy-start | bytes 49156
  0.7 12.9 %copy-start.10 = (bf16[4,2,1024]{2,1,0:T(2,128)(2,1)S(1)}, bf16[4,2,1024]{2,1,0:T(2,128)(2,1)}, u32[]{:S(2)}) copy-start(bf16[4,2,1024]{2,1,0:T(2,128)(2,1)} %param.18) | copy-start | bytes 49156
  0.7 13.0 %copy-start.2 = (bf16[2,128,1024]{2,1,0:T(8,128)(2,1)S(1)}, bf16[2,128,1024]{2,1,0:T(8,128)(2,1)}, u32[]{:S(2)}) copy-start(bf16[2,128,1024]{2,1,0:T(8,128)(2,1)} %value_ref.3) | copy-start | bytes 1572868
  4.6 9.1 %copy-start.1 = (bf16[2,128,1024]{2,1,0:T(8,128)(2,1)S(1)}, bf16[2,128,1024]{2,1,0:T(8,128)(2,1)}, u32[]{:S(2)}) copy-start(bf16[2,128,1024]{2,1,0:T(8,128)(2,1)} %key_ref.3) | copy-start | bytes 1572868
  4.6 11.1 %collective-permute-start = (bf16[8,208,256]{2,1,0:T(8,128)(2,1)}, bf16[8,208,256]{2,1,0:T(8,128)(2,1)S(1)}, u32[]{:S(2)}, u32[]{:S(2)}) collective-permute-start(bf16[8,208,256]{2,1,0:T(8,128)(2,1)} %get-tuple-element.15), channel_id=1, source_target_pairs={{0,1},{1,0},{2,3},{3,2},{4,5},{5,4},{6,7},{7,6},{8,9},{9,8},{10,11... | collective-permute-start | bytes 2555912 | tf_op jit(solution)/shard_map/projection/ppermute | solution.py:365
  13.5 0.7 copy-start.5
  13.5 0.7 copy-start.6
  13.6 2.1 %copy-start = (bf16[8,208,256]{2,1,0:T(8,128)(2,1)S(1)}, bf16[8,208,256]{2,1,0:T(8,128)(2,1)}, u32[]{:S(2)}) copy-start(bf16[8,208,256]{2,1,0:T(8,128)(2,1)} %get-tuple-element.14.mine_ref) | copy-start | bytes 2555908
  16.9 29.1 %copy-start.3 = (f32[2,384,128]{2,1,0:T(8,128)S(1)}, f32[2,384,128]{2,1,0:T(8,128)}, u32[]{:S(2)}) copy-start(f32[2,384,128]{2,1,0:T(8,128)} %constant.22.clone.near_ref) | copy-start | bytes 1179652
  16.9 29.1 %all-to-all-start = ((bf16[8,240,256]{2,1,0:T(8,128)(2,1)}), bf16[8,240,256]{2,1,0:T(8,128)(2,1)S(1)}, u32[]{:S(2)}, u32[]{:S(2)}) async-start(bf16[8,240,256]{2,1,0:T(8,128)(2,1)} %sums.1), calls=%async_computation | async-start | bytes 1966080 | tf_op jit(solution)/shard_map/sums/all_to_all | solution.py:400
  20.6 25.4 %copy-start.4 = (f32[2,8,128]{2,1,0:T(8,128)S(1)}, f32[2,8,128]{2,1,0:T(8,128)}, u32[]{:S(2)}) copy-start(f32[2,8,128]{2,1,0:T(8,128)} %constant.23.clone.far_ref) | copy-start | bytes 24580
  20.6 5.4 %collective-permute-start.1 = (f32[8,512]{1,0:T(8,128)S(1)}, f32[8,512]{1,0:T(8,128)S(1)}, u32[]{:S(2)}, u32[]{:S(2)}) collective-permute-start(f32[8,512]{1,0:T(8,128)S(1)} %constant_dynamic-slice_fusion.query_ref), channel_id=1, source_target_pairs={{0,128},{128,0},{256,384},{384,256},{1,129},{129,1},{257,385},{385... | collective-permute-start | bytes 49160 | tf_op jit(solution)/shard_map/decode_query_exchange/ppermute | solution.py:405
  26.0 9.8 %collective-permute-start.2 = (f32[16,512]{1,0:T(8,128)S(1)}, f32[16,512]{1,0:T(8,128)S(1)}, u32[]{:S(2)}, u32[]{:S(2)}) collective-permute-start(f32[16,512]{1,0:T(8,128)S(1)} %pad_maximum_fusion), channel_id=1, source_target_pairs={{0,256},{128,384},{256,0},{384,128},{1,257},{129,385},{257,1},{385... | collective-permute-start | bytes 98312 | tf_op jit(solution)/shard_map/decode_query_exchange/ppermute | solution.py:406
  47.4 18.0 %all-to-all-start.1 = ((bf16[8,192,256]{2,1,0:T(8,128)(2,1)}), bf16[8,192,256]{2,1,0:T(8,128)(2,1)S(1)}, u32[]{:S(2)}, u32[]{:S(2)}) async-start(bf16[8,192,256]{2,1,0:T(8,128)(2,1)} %get-tuple-element.20), calls=%async_computation.1 | async-start | bytes 1572864 | tf_op jit(solution)/shard_map/share/all_to_all | solution.py:422
  53.5 3.5 %collective-permute-start.3 = (f32[32,256]{1,0:T(8,128)S(1)}, f32[32,256]{1,0:T(8,128)S(1)}, u32[]{:S(2)}, u32[]{:S(2)}) collective-permute-start(f32[32,256]{1,0:T(8,128)S(1)} %get-tuple-element.21), channel_id=1, source_target_pairs={{0,1},{1,0},{2,3},{3,2},{4,5},{5,4},{6,7},{7,6},{8,9},{9,8},{10,11... | collective-permute-start | bytes 98312 | tf_op jit(solution)/shard_map/share/ppermute | solution.py:423
  65.4 16.6 %copy-start.7 = (bf16[1,384,512]{2,1,0:T(8,128)(2,1)S(1)}, bf16[1,384,512]{2,1,0:T(8,128)(2,1)}, u32[]{:S(2)}) copy-start(bf16[1,384,512]{2,1,0:T(8,128)(2,1)} %param.14) | copy-start | bytes 1179652
  65.4 5.9 %collective-permute-start.4 = (bf16[1536,256]{1,0:T(8,128)(2,1)S(1)}, bf16[1536,256]{1,0:T(8,128)(2,1)S(1)}, u32[]{:S(2)}, u32[]{:S(2)}) collective-permute-start(bf16[1536,256]{1,0:T(8,128)(2,1)S(1)} %bitcast.4), channel_id=1, source_target_pairs={{0,1},{1,0},{2,3},{3,2},{4,5},{5,4},{6,7},{7,6},{8,9},{9,8},{10,11... | collective-permute-start | bytes 2359304 | tf_op jit(solution)/shard_map/passage_rows/ppermute | solution.py:427
  72.9 16.5 %all-to-all-start.2 = ((f32[4,32,256]{2,1,0:T(8,128)}), f32[4,32,256]{2,1,0:T(8,128)S(1)}, u32[]{:S(2)}, u32[]{:S(2)}) async-start(f32[4,32,256]{2,1,0:T(8,128)} %passage_rows.1), calls=%async_computation.2 | async-start | bytes 262144 | tf_op jit(solution)/shard_map/passage_rows/all_to_all | solution.py:440

commit v4 on v3

--- a/solution.py
+++ b/solution.py
@@ -212,31 +212,34 @@
         ).astype(bf16)
 
 
-def passage_states(
-    query_ref, query1_ref, query2_ref, own_ref, other_ref, out_ref
-):
+def passage_states(query_ref, query1_ref, query2_ref, kv_ref, out_ref):
+    heads = 2 * HEADS
     queries = [query_ref[...], query1_ref[...], query2_ref[:8, :], query2_ref[8:, :]]
     query = jnp.concatenate(
-        [rows[:, p * HS : (p + 1) * HS] for rows in queries for p in range(HEADS)], axis=0
+        [rows[:, p * HS : (p + 1) * HS] for rows in queries for p in range(heads)], axis=0
     ).astype(bf16)
-    refs = (own_ref, other_ref)
-    scores = [dot_t(query, ref[:, :HS]) * SCALE2 for ref in refs]
-    highest = jnp.max(jnp.maximum(*scores), axis=1, keepdims=True)
-    weights = [jnp.exp2(score - highest) for score in scores]
-    totals = jnp.sum(weights[0] + weights[1], axis=1, keepdims=True)
-    weighted = sum(dot(w.astype(bf16), ref[:, HS:]) for w, ref in zip(weights, refs, strict=True))
+    scores = dot_t(query, kv_ref[:, :HS]) * SCALE2
+    highest = jnp.max(scores, axis=1, keepdims=True)
+    weights = jnp.exp2(scores - highest)
+    totals = jnp.sum(weights, axis=1, keepdims=True)
+    weighted = dot(weights.astype(bf16), kv_ref[:, HS:])
     state = state_of(weighted, highest, totals)
     for r in range(4):
-        out_ref[lax.axis_index("group") ^ r] = state[32 * r : 32 * (r + 1)]
-
-
-def attend(query_ref, near_ref, far_ref, own_ref, other_ref, out_ref, turned_ref, values_ref):
-    s, core = lax.axis_index("seq"), lax.axis_index("core")
-    cosine, sine = turn_by(near_ref, far_ref, s, slice(None))
+        for core in range(2):
+            at = (2 * r + core) * 32
+            out_ref[2 * (lax.axis_index("group") ^ r) + core] = state[at : at + 32]
+
+
+def turn_queries(query_ref, near_ref, far_ref, out_ref):
+    cosine, sine = turn_by(near_ref, far_ref, lax.axis_index("seq"), slice(None))
     cosine, sine = cosine * SCALE2, sine * SCALE2
     for h in range(HEADS):
         x = query_ref[:, h * HS : (h + 1) * HS].astype(f32)
-        turned_ref[h] = turned(x, cosine, sine).astype(bf16)
+        out_ref[h] = turned(x, cosine, sine).astype(bf16)
+
+
+def attend(turned_ref, own_ref, other_ref, out_ref, values_ref):
+    s, core = lax.axis_index("seq"), lax.axis_index("core")
 
     def run(pairs):
         keys = pairs * TOK
@@ -278,10 +281,12 @@
 
 def merge(chosen_ref, passages_ref, cache_ref, other_ref, out_ref):
     chosen = chosen_ref[...]
-    state = passages_ref[0]
-    for g in range(1, passages_ref.shape[0]):
-        state = jnp.where(chosen == g, passages_ref[g], state)
-    weighted, _, total = parts_of(merged(state, merged(cache_ref[...], other_ref[...])))
+    states = [passages_ref[0], passages_ref[1]]
+    for g in range(1, passages_ref.shape[0] // 2):
+        for core in range(2):
+            states[core] = jnp.where(chosen == g, passages_ref[2 * g + core], states[core])
+    states += [cache_ref[...], other_ref[...]]
+    weighted, _, total = parts_of(merged(merged(*states[:2]), merged(*states[2:])))
     context = weighted / total
     for step in range(out_ref.shape[0]):
         for p in range(HEADS):
@@ -322,7 +327,6 @@
 ):
     near, far = tables()
     groups = lax.axis_size("group")
-    tp = lax.axis_index("y") * 2 + lax.axis_index("core")
     features = hidden.shape[2]
     swap = [(0, 1), (1, 0)]
     state = (32, 2 * HS)
@@ -401,14 +405,27 @@
 
     with jax.named_scope("decode_query_exchange"):
         queries, _ = lax.optimization_barrier((queries, chunks))
-        own = lax.dynamic_slice_in_dim(queries, tp * HEADS * HS, HEADS * HS, 1)
+        own = lax.dynamic_slice_in_dim(queries, lax.axis_index("y") * 8 * HS, 8 * HS, 1)
         near_group = lax.ppermute(own, "group", [(g, g ^ 1) for g in range(groups)])
         far_groups = lax.ppermute(
             jnp.concatenate([own, near_group]), "group", [(g, g ^ 2) for g in range(groups)]
         )
 
     with jax.named_scope("share"):
-        sums, far_groups = lax.optimization_barrier((sums, far_groups))
+        queries, _ = lax.optimization_barrier((passage_queries[0], chunks))
+        turned_queries = call(
+            turn_queries,
+            shape((HEADS, TOK, HS), bf16),
+            0,
+            3,
+            queries,
+            near,
+            far,
+            cost_estimate=cost(1 << 20),
+        )
+        sums, far_groups, turned_queries = lax.optimization_barrier(
+            (sums, far_groups, turned_queries)
+        )
         share, keep, send = call(
             finish_share,
             [shape((SEQ, HALF, 2 * HS), bf16), shape(state, f32), shape(state, f32)],
@@ -427,38 +444,33 @@
         other_kv = lax.ppermute(own_kv, "core", swap)
         rows_passage = call(
             passage_states,
-            shape((groups, *state), f32),
+            shape((2 * groups, *state), f32),
             0,
-            5,
+            4,
             own,
             near_group,
             far_groups,
             own_kv,
-            other_kv,
-            cost_estimate=cost(128 * 3072 * 128 * 4, 128 * 3072, 2 << 20),
-        )
-        returned = lax.all_to_all(rows_passage, "group", 0, 0, tiled=True)
+            cost_estimate=cost(256 * 1536 * 128 * 4, 256 * 1536, 2 << 20),
+        )
+        returned = lax.all_to_all(rows_passage, ("group", "core"), 0, 0, tiled=True)
 
     with jax.named_scope("passage_attention"):
         passage_out = call(
             attend,
             shape((TOK, HEADS * HS), bf16),
             0,
-            5,
-            passage_queries[0],
-            near,
-            far,
+            3,
+            turned_queries,
             own_kv,
             other_kv,
             mib=48,
-            scratch_shapes=[
-                pltpu.VMEM((HEADS, TOK, HS), bf16),
-                pltpu.VMEM((2, SEQ * HALF, 2 * HS), bf16),
-            ],
+            scratch_shapes=[pltpu.VMEM((2, SEQ * HALF, 2 * HS), bf16)],
             cost_estimate=cost(1536 * 3072 * 128 * 4 * 4, 1536 * 3072, 3 << 20),
         )
 
     with jax.named_scope("row_merge"):
+        chosen, passage_out = lax.optimization_barrier((chosen, passage_out))
         row_out = call(
             merge,
             shape((4, 2, HEADS * HS), bf16),

time: 90.9 us -> 92.3 us (1.015)
  Pallas kernels: 14.2 us -> 15.4 us
    all_to_all x1, waiting for transfers between devices: 3.61 us -> 5.71 us  [per_device(): returned = lax.all_to_all(rows_passage, ('group', 'core'), 0, 0, tiled=True)]
    ppermute x1, waiting for transfers between devices: 1.89 us -> 0.01 us  [per_device(): other_kv = lax.ppermute(own_kv, 'core', swap)]
    pallas_call x6 -> x7, Pallas kernels: 10.3 us -> 11.5 us  [call(): pl.pallas_call(kernel, in_specs=smem(scalars) + vmem(arrays), out_specs=v...]
  transfers between devices with their start and end apart: 8 -> 8, of which waited for: 8 -> 7; matrix products, arithmetic and copies ran while one was open for 0% -> 0% of each run, Pallas kernels for 6% -> 9%
where the time goes in v4:
time: 92.3 us; the launch traced here: 91.7 us
  starting transfers between devices  46.9 us (51%)
  waiting for transfers between devices  28 us (30%)
  Pallas kernels  15.4 us (17%)
    pallas_call x7, Pallas kernels, call(): pl.pallas_call(kernel, in_specs=smem(scalars) + vmem(arrays), out_specs=v...  11.5 us
    all_to_all x1, waiting for transfers between devices, per_device(): sums = lax.all_to_all(chunks, 'y', 0, 0, tiled=True)  9.63 us
    all_to_all x1, starting transfers between devices, per_device(): returned = lax.all_to_all(rows_passage, ('group', 'core'), 0, 0, tiled=True)  9.52 us
    ppermute x1, starting transfers between devices, per_device(): theirs = lax.ppermute(theirs, 'core', swap)  8.91 us
    ppermute x1, starting transfers between devices, per_device(): lax.ppermute(jnp.concatenate([own, near_group]), 'group', [(g, g ^ 2) for...  8.49 us
    all_to_all x1, waiting for transfers between devices, per_device(): received = lax.all_to_all(share, 'seq', 0, 0, tiled=True)  8.37 us
    all_to_all x1, starting transfers between devices, per_device(): received = lax.all_to_all(share, 'seq', 0, 0, tiled=True)  6.07 us
    all_to_all x1, waiting for transfers between devices, per_device(): returned = lax.all_to_all(rows_passage, ('group', 'core'), 0, 0, tiled=True)  5.71 us
  transfers between devices with their start and end apart: 8, of which 7 were waited for; matrix products, arithmetic and copies ran while one was open for 0% of the time, Pallas kernels for 9%

profile of v4, /device:TPU:1, one launch (start us, length us, event | category | flops | bytes accessed | tf_op | source)
XLA Modules:
  0.0 91.7 jit_solution(13157713695614563219)
XLA Ops:
  0.6 0.0 copy-start.8
  0.6 0.0 copy-start.9
  0.7 0.0 copy-start.10
  0.7 3.9 %projection.1 = (bf16[8,208,256]{2,1,0:T(8,128)(2,1)}, bf16[8,208,256]{2,1,0:T(8,128)(2,1)}) custom-call(bf16[384,512]{1,0:T(8,128)(2,1)} %bitcast.8, bf16[512,1024]{1,0:T(8,128)(2,1)} %key_ref.3, bf16[512,1024]{1,0:T(8,128)(2,1)} %value_ref.3), custom_call_target="tpu_custom_call" | custom-call | flops 805306368 | bytes 4194304 | tf_op jit(solution)/shard_map/projection/pallas_call | solution.py:352
  4.6 8.9 %collective-permute-start = (bf16[8,208,256]{2,1,0:T(8,128)(2,1)}, bf16[8,208,256]{2,1,0:T(8,128)(2,1)S(1)}, u32[]{:S(2)}, u32[]{:S(2)}) collective-permute-start(bf16[8,208,256]{2,1,0:T(8,128)(2,1)} %get-tuple-element.20), channel_id=1, source_target_pairs={{0,1},{1,0},{2,3},{3,2},{4,5},{5,4},{6,7},{7,6},{8,9},{9,8},{10,11... | collective-permute-start | bytes 2555912 | tf_op jit(solution)/shard_map/projection/ppermute | solution.py:369
  13.5 0.0 copy-start.6
  13.5 0.0 copy-start.7
  13.7 0.4 copy-done.6
  14.1 0.0 copy-done.7
  14.2 1.4 %cache.1 = (bf16[8,32,256]{2,1,0:T(8,128)(2,1)S(1)}, bf16[8,16,256]{2,1,0:T(8,128)(2,1)S(1)}, s32[32,256]{1,0:T(8,128)S(1)}) custom-call(s32[2]{0:T(128)S(1)} %copy-done.6, s32[2]{0:T(128)S(1)} %copy-done.7, f32[8,8192]{1,0:T(8,128)S(1)} %reshape.14.query_ref, f32[8,2048]{1,0:T(8,128)S(1)} %reshape.15.new_ref, bf16[2,128,1024]{2,1,0:T(8,128)(2,1)S(1)} %copy-done.2, ...), custom_call_target="tpu_custom_call" | custom-call | flops 67108864 | bytes 2097152 | tf_op jit(solution)/shard_map/cache/pallas_call | solution.py:336
  15.5 0.1 collective-permute-done.other_ref
  15.7 1.2 %sums.1 = bf16[8,240,256]{2,1,0:T(8,128)(2,1)} custom-call(bf16[8,208,256]{2,1,0:T(8,128)(2,1)S(1)} %copy-done.1, bf16[8,208,256]{2,1,0:T(8,128)(2,1)S(1)} %collective-permute-done.other_ref, bf16[8,32,256]{2,1,0:T(8,128)(2,1)S(1)} %get-tuple-element.21.cache_ref, bf16[8,16,256]{2,1,0:T(8,128)(2,1)S(1)} %get-tuple-element.22.tail_ref), custom_call_target="tpu_custom_call" | custom-call | flops 1048576 | bytes 1048576 | tf_op jit(solution)/shard_map/sums/pallas_call | solution.py:336
  16.9 3.7 %all-to-all-start = ((bf16[8,240,256]{2,1,0:T(8,128)(2,1)}), bf16[8,240,256]{2,1,0:T(8,128)(2,1)S(1)}, u32[]{:S(2)}, u32[]{:S(2)}) async-start(bf16[8,240,256]{2,1,0:T(8,128)(2,1)} %sums.1), calls=%async_computation | async-start | bytes 1966080 | tf_op jit(solution)/shard_map/sums/all_to_all | solution.py:404
  20.6 0.0 copy-start.5
  20.6 3.7 %collective-permute-start.1 = (f32[8,1024]{1,0:T(8,128)S(1)}, f32[8,1024]{1,0:T(8,128)S(1)}, u32[]{:S(2)}, u32[]{:S(2)}) collective-permute-start(f32[8,1024]{1,0:T(8,128)S(1)} %constant_dynamic-slice_fusion.query_ref), channel_id=1, source_target_pairs={{0,128},{128,0},{256,384},{384,256},{1,129},{129,1},{257,385},{385... | collective-permute-start | bytes 98312 | tf_op jit(solution)/shard_map/decode_query_exchange/ppermute | solution.py:409
  24.3 1.9 %collective-permute-done.1.query1_ref = f32[8,1024]{1,0:T(8,128)S(1)} collective-permute-done((f32[8,1024]{1,0:T(8,128)S(1)}, f32[8,1024]{1,0:T(8,128)S(1)}, u32[]{:S(2)}, u32[]{:S(2)}) %collective-permute-start.1) | collective-permute-done | bytes 32800 | tf_op jit(solution)/shard_map/decode_query_exchange/ppermute | solution.py:409
  26.2 8.5 %collective-permute-start.2 = (f32[16,1024]{1,0:T(8,128)S(1)}, f32[16,1024]{1,0:T(8,128)S(1)}, u32[]{:S(2)}, u32[]{:S(2)}) collective-permute-start(f32[16,1024]{1,0:T(8,128)S(1)} %pad_maximum_fusion), channel_id=1, source_target_pairs={{0,256},{128,384},{256,0},{384,128},{1,257},{129,385},{257,1},{385... | collective-permute-start | bytes 196616 | tf_op jit(solution)/shard_map/decode_query_exchange/ppermute | solution.py:410
  34.7 0.3 share.2.turned_ref
  35.0 1.4 %collective-permute-done.2.query2_ref = f32[16,1024]{1,0:T(8,128)S(1)} collective-permute-done((f32[16,1024]{1,0:T(8,128)S(1)}, f32[16,1024]{1,0:T(8,128)S(1)}, u32[]{:S(2)}, u32[]{:S(2)}) %collective-permute-start.2) | collective-permute-done | bytes 65568 | tf_op jit(solution)/shard_map/decode_query_exchange/ppermute | solution.py:410
  36.4 9.6 %all-to-all-done.sums_ref = bf16[8,240,256]{2,1,0:T(8,128)(2,1)S(1)} async-done(((bf16[8,240,256]{2,1,0:T(8,128)(2,1)}), bf16[8,240,256]{2,1,0:T(8,128)(2,1)S(1)}, u32[]{:S(2)}, u32[]{:S(2)}) %all-to-all-start) | async-done | bytes 983072 | tf_op jit(solution)/shard_map/sums/all_to_all | solution.py:404
  46.0 1.4 %share.3 = (bf16[8,192,256]{2,1,0:T(8,128)(2,1)}, f32[32,256]{1,0:T(8,128)S(1)}, f32[32,256]{1,0:T(8,128)S(1)}) custom-call(bf16[8,240,256]{2,1,0:T(8,128)(2,1)S(1)} %all-to-all-done.sums_ref, f32[2,384,128]{2,1,0:T(8,128)S(1)} %copy-done, f32[2,8,128]{2,1,0:T(8,128)S(1)} %copy-done.5), custom_call_target="tpu_custom_call" | custom-call | flops 1048576 | bytes 1048576 | tf_op jit(solution)/shard_map/share/pallas_call | solution.py:336
  47.4 6.1 %all-to-all-start.1 = ((bf16[8,192,256]{2,1,0:T(8,128)(2,1)}), bf16[8,192,256]{2,1,0:T(8,128)(2,1)S(1)}, u32[]{:S(2)}, u32[]{:S(2)}) async-start(bf16[8,192,256]{2,1,0:T(8,128)(2,1)} %get-tuple-element.27), calls=%async_computation.1 | async-start | bytes 1572864 | tf_op jit(solution)/shard_map/share/all_to_all | solution.py:439
  53.5 2.7 %collective-permute-start.3 = (f32[32,256]{1,0:T(8,128)S(1)}, f32[32,256]{1,0:T(8,128)S(1)}, u32[]{:S(2)}, u32[]{:S(2)}) collective-permute-start(f32[32,256]{1,0:T(8,128)S(1)} %get-tuple-element.28), channel_id=1, source_target_pairs={{0,1},{1,0},{2,3},{3,2},{4,5},{5,4},{6,7},{7,6},{8,9},{9,8},{10,11... | collective-permute-start | bytes 98312 | tf_op jit(solution)/shard_map/share/ppermute | solution.py:440
  56.2 0.8 collective-permute-done.3.other_ref
  57.0 8.4 %all-to-all-done.1 = bf16[8,192,256]{2,1,0:T(8,128)(2,1)S(1)} async-done(((bf16[8,192,256]{2,1,0:T(8,128)(2,1)}), bf16[8,192,256]{2,1,0:T(8,128)(2,1)S(1)}, u32[]{:S(2)}, u32[]{:S(2)}) %all-to-all-start.1) | async-done | bytes 786464 | tf_op jit(solution)/shard_map/share/all_to_all | solution.py:439
  65.4 3.9 %collective-permute-start.4 = (bf16[1536,256]{1,0:T(8,128)(2,1)S(1)}, bf16[1536,256]{1,0:T(8,128)(2,1)}, u32[]{:S(2)}, u32[]{:S(2)}) collective-permute-start(bf16[1536,256]{1,0:T(8,128)(2,1)S(1)} %bitcast.4), channel_id=1, source_target_pairs={{0,1},{1,0},{2,3},{3,2},{4,5},{5,4},{6,7},{7,6},{8,9},{9,8},{10,11... | collective-permute-start | bytes 2359304 | tf_op jit(solution)/shard_map/passage_rows/ppermute | solution.py:444
  69.3 1.6 %passage_rows.1 = f32[8,32,256]{2,1,0:T(8,128)} custom-call(f32[8,1024]{1,0:T(8,128)S(1)} %constant_dynamic-slice_fusion.query_ref, f32[8,1024]{1,0:T(8,128)S(1)} %collective-permute-done.1.query1_ref, f32[16,1024]{1,0:T(8,128)S(1)} %collective-permute-done.2.query2_ref, bf16[1536,256]{1,0:T(8,128)(2,1)S(1)} %bitcast.5), custom_call_target="tpu_custom_call" | custom-call | flops 201326592 | bytes 2097152 | tf_op jit(solution)/shard_map/passage_rows/pallas_call | solution.py:336
  70.9 9.5 %all-to-all-start.2 = ((f32[8,32,256]{2,1,0:T(8,128)}), f32[8,32,256]{2,1,0:T(8,128)S(1)}, u32[]{:S(2)}, u32[]{:S(2)}) async-start(f32[8,32,256]{2,1,0:T(8,128)} %passage_rows.1), calls=%async_computation.2 | async-start | bytes 524288 | tf_op jit(solution)/shard_map/passage_rows/all_to_all | solution.py:456
  80.4 0.0 collective-permute-done.4.other_ref
  80.4 4.6 %passage_attention.1 = bf16[384,512]{1,0:T(8,128)(2,1)} custom-call(bf16[4,384,128]{2,1,0:T(8,128)(2,1)S(1)} %share.2.turned_ref, bf16[1536,256]{1,0:T(8,128)(2,1)S(1)} %bitcast.6, bf16[1536,256]{1,0:T(8,128)(2,1)} %collective-permute-done.4.other_ref), custom_call_target="tpu_custom_call" | custom-call | flops 9663676416 | bytes 3145728 | tf_op jit(solution)/shard_map/passage_attention/pallas_call | solution.py:336
  85.0 5.7 %all-to-all-done.2.passages_ref = f32[8,32,256]{2,1,0:T(8,128)S(1)} async-done(((f32[8,32,256]{2,1,0:T(8,128)}), f32[8,32,256]{2,1,0:T(8,128)S(1)}, u32[]{:S(2)}, u32[]{:S(2)}) %all-to-all-start.2) | async-done | bytes 262176 | tf_op jit(solution)/shard_map/passage_rows/all_to_all | solution.py:456
  90.7 1.0 %row_merge.1 = bf16[4,2,512]{2,1,0:T(2,128)(2,1)} custom-call(s32[32,256]{1,0:T(8,128)S(1)} %get-tuple-element.31.chosen_ref, f32[8,32,256]{2,1,0:T(8,128)S(1)} %all-to-all-done.2.passages_ref, f32[32,256]{1,0:T(8,128)S(1)} %get-tuple-element.33.cache_ref, f32[32,256]{1,0:T(8,128)S(1)} %collective-permute-done.3.other_ref), custom_call_target="tpu_custom_call" | custom-call | flops 1048576 | bytes 1048576 | tf_op jit(solution)/shard_map/row_merge/pallas_call | solution.py:336
  (19 shorter events, 0.2 us)
Async XLA Ops:
  0.6 12.9 %copy-start.8 = (bf16[4,2,8192]{2,1,0:T(2,128)(2,1)S(1)}, bf16[4,2,8192]{2,1,0:T(2,128)(2,1)}, u32[]{:S(2)}) copy-start(bf16[4,2,8192]{2,1,0:T(2,128)(2,1)} %param.17) | copy-start | bytes 393220
  0.6 12.9 %copy-start.9 = (bf16[4,2,1024]{2,1,0:T(2,128)(2,1)S(1)}, bf16[4,2,1024]{2,1,0:T(2,128)(2,1)}, u32[]{:S(2)}) copy-start(bf16[4,2,1024]{2,1,0:T(2,128)(2,1)} %param.19) | copy-start | bytes 49156
  0.7 12.9 %copy-start.10 = (bf16[4,2,1024]{2,1,0:T(2,128)(2,1)S(1)}, bf16[4,2,1024]{2,1,0:T(2,128)(2,1)}, u32[]{:S(2)}) copy-start(bf16[4,2,1024]{2,1,0:T(2,128)(2,1)} %param.18) | copy-start | bytes 49156
  0.7 13.0 %copy-start.3 = (bf16[2,128,1024]{2,1,0:T(8,128)(2,1)S(1)}, bf16[2,128,1024]{2,1,0:T(8,128)(2,1)}, u32[]{:S(2)}) copy-start(bf16[2,128,1024]{2,1,0:T(8,128)(2,1)} %value_ref.2) | copy-start | bytes 1572868
  4.6 9.1 %copy-start.2 = (bf16[2,128,1024]{2,1,0:T(8,128)(2,1)S(1)}, bf16[2,128,1024]{2,1,0:T(8,128)(2,1)}, u32[]{:S(2)}) copy-start(bf16[2,128,1024]{2,1,0:T(8,128)(2,1)} %key_ref.2) | copy-start | bytes 1572868
  4.6 11.1 %collective-permute-start = (bf16[8,208,256]{2,1,0:T(8,128)(2,1)}, bf16[8,208,256]{2,1,0:T(8,128)(2,1)S(1)}, u32[]{:S(2)}, u32[]{:S(2)}) collective-permute-start(bf16[8,208,256]{2,1,0:T(8,128)(2,1)} %get-tuple-element.20), channel_id=1, source_target_pairs={{0,1},{1,0},{2,3},{3,2},{4,5},{5,4},{6,7},{7,6},{8,9},{9,8},{10,11... | collective-permute-start | bytes 2555912 | tf_op jit(solution)/shard_map/projection/ppermute | solution.py:369
  13.5 0.7 copy-start.6
  13.5 0.7 copy-start.7
  13.6 2.1 %copy-start.1 = (bf16[8,208,256]{2,1,0:T(8,128)(2,1)S(1)}, bf16[8,208,256]{2,1,0:T(8,128)(2,1)}, u32[]{:S(2)}) copy-start(bf16[8,208,256]{2,1,0:T(8,128)(2,1)} %get-tuple-element.19.mine_ref) | copy-start | bytes 2555908
  16.9 17.8 %copy-start = (f32[2,384,128]{2,1,0:T(8,128)S(1)}, f32[2,384,128]{2,1,0:T(8,128)}, u32[]{:S(2)}) copy-start(f32[2,384,128]{2,1,0:T(8,128)} %constant.18.clone.near_ref) | copy-start | bytes 1179652
  16.9 17.8 %copy-start.4 = (bf16[1,384,512]{2,1,0:T(8,128)(2,1)S(1)}, bf16[1,384,512]{2,1,0:T(8,128)(2,1)}, u32[]{:S(2)}) copy-start(bf16[1,384,512]{2,1,0:T(8,128)(2,1)} %param.14) | copy-start | bytes 1179652
  16.9 29.1 %all-to-all-start = ((bf16[8,240,256]{2,1,0:T(8,128)(2,1)}), bf16[8,240,256]{2,1,0:T(8,128)(2,1)S(1)}, u32[]{:S(2)}, u32[]{:S(2)}) async-start(bf16[8,240,256]{2,1,0:T(8,128)(2,1)} %sums.1), calls=%async_computation | async-start | bytes 1966080 | tf_op jit(solution)/shard_map/sums/all_to_all | solution.py:404
  20.6 14.1 %copy-start.5 = (f32[2,8,128]{2,1,0:T(8,128)S(1)}, f32[2,8,128]{2,1,0:T(8,128)}, u32[]{:S(2)}) copy-start(f32[2,8,128]{2,1,0:T(8,128)} %constant.19.clone.far_ref) | copy-start | bytes 24580
  20.6 5.6 %collective-permute-start.1 = (f32[8,1024]{1,0:T(8,128)S(1)}, f32[8,1024]{1,0:T(8,128)S(1)}, u32[]{:S(2)}, u32[]{:S(2)}) collective-permute-start(f32[8,1024]{1,0:T(8,128)S(1)} %constant_dynamic-slice_fusion.query_ref), channel_id=1, source_target_pairs={{0,128},{128,0},{256,384},{384,256},{1,129},{129,1},{257,385},{385... | collective-permute-start | bytes 98312 | tf_op jit(solution)/shard_map/decode_query_exchange/ppermute | solution.py:409
  26.2 10.2 %collective-permute-start.2 = (f32[16,1024]{1,0:T(8,128)S(1)}, f32[16,1024]{1,0:T(8,128)S(1)}, u32[]{:S(2)}, u32[]{:S(2)}) collective-permute-start(f32[16,1024]{1,0:T(8,128)S(1)} %pad_maximum_fusion), channel_id=1, source_target_pairs={{0,256},{128,384},{256,0},{384,128},{1,257},{129,385},{257,1},{385... | collective-permute-start | bytes 196616 | tf_op jit(solution)/shard_map/decode_query_exchange/ppermute | solution.py:410
  47.4 18.0 %all-to-all-start.1 = ((bf16[8,192,256]{2,1,0:T(8,128)(2,1)}), bf16[8,192,256]{2,1,0:T(8,128)(2,1)S(1)}, u32[]{:S(2)}, u32[]{:S(2)}) async-start(bf16[8,192,256]{2,1,0:T(8,128)(2,1)} %get-tuple-element.27), calls=%async_computation.1 | async-start | bytes 1572864 | tf_op jit(solution)/shard_map/share/all_to_all | solution.py:439
  53.5 3.5 %collective-permute-start.3 = (f32[32,256]{1,0:T(8,128)S(1)}, f32[32,256]{1,0:T(8,128)S(1)}, u32[]{:S(2)}, u32[]{:S(2)}) collective-permute-start(f32[32,256]{1,0:T(8,128)S(1)} %get-tuple-element.28), channel_id=1, source_target_pairs={{0,1},{1,0},{2,3},{3,2},{4,5},{5,4},{6,7},{7,6},{8,9},{9,8},{10,11... | collective-permute-start | bytes 98312 | tf_op jit(solution)/shard_map/share/ppermute | solution.py:440
  65.4 15.0 %collective-permute-start.4 = (bf16[1536,256]{1,0:T(8,128)(2,1)S(1)}, bf16[1536,256]{1,0:T(8,128)(2,1)}, u32[]{:S(2)}, u32[]{:S(2)}) collective-permute-start(bf16[1536,256]{1,0:T(8,128)(2,1)S(1)} %bitcast.4), channel_id=1, source_target_pairs={{0,1},{1,0},{2,3},{3,2},{4,5},{5,4},{6,7},{7,6},{8,9},{9,8},{10,11... | collective-permute-start | bytes 2359304 | tf_op jit(solution)/shard_map/passage_rows/ppermute | solution.py:444
  70.9 19.8 %all-to-all-start.2 = ((f32[8,32,256]{2,1,0:T(8,128)}), f32[8,32,256]{2,1,0:T(8,128)S(1)}, u32[]{:S(2)}, u32[]{:S(2)}) async-start(f32[8,32,256]{2,1,0:T(8,128)} %passage_rows.1), calls=%async_computation.2 | async-start | bytes 524288 | tf_op jit(solution)/shard_map/passage_rows/all_to_all | solution.py:456
